TPU v7x, 32 devices: a whole 2x2x4 slice. The times are simulated.
32 devices in a mesh: gx: 2 (over y), gy: 4 (over x, core), gz: 4 (over z).
Axes of the slice: x: 2, y: 2, z: 4, core: 2. Of those that a mesh axis runs over, the one named last changes fastest.
Arguments:
- element_load: float32 [20, 68, 256], P('gz', 'gy', 'gx'), may hold values from -6 to 6
- conductivity: float32 [8, 32, 128], P('gz', 'gy', 'gx'), may hold values from 0.2 to 5
Outputs:
- corrected: float32 [20, 68, 256], P('gz', 'gy', 'gx')
All inputs are finite; a program needn't handle non-finite values.
Results may differ from a plain program's by a relative error of at most 0.00002.
Values sent between devices are 32-bit elements; how exact they have to be, the bound alone decides.
A program may use at most 64 MiB of HBM per device.

v0:
```python
import jax
import jax.numpy as jnp
import numpy as np
from jax import lax
from jax.sharding import PartitionSpec as P

DEG1 = 3
DEG2 = 4


reaction_rate = 0.05
lower_bound = 0.25
upper_bound = 2.5
mass_table = [
    [4.0 / 30.0, 2.0 / 30.0, -1.0 / 30.0],
    [2.0 / 30.0, 16.0 / 30.0, 2.0 / 30.0],
    [-1.0 / 30.0, 2.0 / 30.0, 4.0 / 30.0],
]
stiff_table = [
    [7.0 / 3.0, -8.0 / 3.0, 1.0 / 3.0],
    [-8.0 / 3.0, 16.0 / 3.0, -8.0 / 3.0],
    [1.0 / 3.0, -8.0 / 3.0, 7.0 / 3.0],
]


def padded(cells, sides, width):
    for axis, dim in sides:
        count = lax.axis_size(axis)
        head = lax.slice_in_dim(cells, 0, width, axis=dim)
        tail = lax.slice_in_dim(cells, cells.shape[dim] - width, cells.shape[dim], axis=dim)
        cells = jnp.concatenate(
            [
                lax.ppermute(tail, axis, [(i, (i + 1) % count) for i in range(count)]),
                cells,
                lax.ppermute(head, axis, [((i + 1) % count, i) for i in range(count)]),
            ],
            axis=dim,
        )
    return cells


def pad_axis(values, which_axis, before, after):
    widths = [(0, 0)] * values.ndim
    widths[which_axis] = (before, after)
    return jnp.pad(values, widths)


def contract(values, matrix, which_axis):
    pieces = [lax.index_in_dim(values, a, which_axis, keepdims=False) for a in range(3)]
    results = [
        matrix[b][0] * pieces[0] + matrix[b][1] * pieces[1] + matrix[b][2] * pieces[2]
        for b in range(3)
    ]
    return jnp.stack(results, axis=which_axis)


def node_slices(node_field, which_axis, periodic):
    if periodic:
        length_here = node_field.shape[which_axis]
        even_nodes = lax.slice_in_dim(node_field, 0, length_here, 2, axis=which_axis)
        odd_nodes = lax.slice_in_dim(node_field, 1, length_here, 2, axis=which_axis)
        return [even_nodes, odd_nodes, jnp.roll(even_nodes, -1, axis=which_axis)]
    elements = (node_field.shape[which_axis] - 1) // 2
    return [
        lax.slice_in_dim(node_field, a, a + 2 * elements - 1, 2, axis=which_axis) for a in range(3)
    ]


def spread(node_field, periodic):
    along_x = jnp.stack(node_slices(node_field, 2, periodic), 0)
    along_y = jnp.stack(node_slices(along_x, 2, False), 1)
    return jnp.stack(node_slices(along_y, 2, False), 2)


def fold_back(stacked, which_axis, periodic):
    lower_part = stacked[0]
    middle_part = stacked[1]
    upper_part = stacked[2]
    target = which_axis - 1
    elements = lower_part.shape[target]
    if periodic:
        even_nodes = lower_part + jnp.roll(upper_part, 1, axis=target)
    else:
        even_full = pad_axis(lower_part, target, 0, 1) + pad_axis(upper_part, target, 1, 0)
        even_nodes = lax.slice_in_dim(even_full, 0, elements, axis=target)
        tail_node = lax.slice_in_dim(even_full, elements, elements + 1, axis=target)
    woven_nodes = jnp.stack([even_nodes, middle_part], axis=target + 1)
    node_shape = list(even_nodes.shape)
    node_shape[target] = 2 * elements
    woven_nodes = woven_nodes.reshape(node_shape)
    if periodic:
        return woven_nodes
    return jnp.concatenate([woven_nodes, tail_node], axis=target)


def gather_elements(product, periodic):
    folded = fold_back(product, 5, periodic)
    folded = fold_back(folded, 3, False)
    return fold_back(folded, 1, False)


def apply_local(node_field, conduct, stiff_scale, mass_scale, periodic):
    node_values = spread(node_field, periodic)
    mass_depth = contract(node_values, mass_table, 2)
    mass_plane = contract(mass_depth, mass_table, 1)
    stiffness = contract(mass_plane, stiff_table, 0)
    mass_width = contract(node_values, mass_table, 0)
    stiffness = stiffness + contract(contract(mass_width, stiff_table, 1), mass_table, 2)
    mass_face = contract(mass_width, mass_table, 1)
    stiffness = stiffness + contract(mass_face, stiff_table, 2)
    product = stiff_scale * conduct * stiffness + mass_scale * contract(mass_face, mass_table, 2)
    return gather_elements(product, periodic)


def diag_tables():
    stiff_line = np.array([stiff_table[a][a] for a in range(3)])
    mass_line = np.array([mass_table[a][a] for a in range(3)])
    stiff_part = (
        stiff_line[:, None, None] * mass_line[None, :, None] * mass_line[None, None, :]
        + mass_line[:, None, None] * stiff_line[None, :, None] * mass_line[None, None, :]
        + mass_line[:, None, None] * mass_line[None, :, None] * stiff_line[None, None, :]
    )
    mass_part = mass_line[:, None, None] * mass_line[None, :, None] * mass_line[None, None, :]
    return (stiff_part.reshape(3, 3, 3, 1, 1, 1), mass_part.reshape(3, 3, 3, 1, 1, 1))


def diag_local(conduct, stiff_scale, mass_scale):
    stiff_part, mass_part = diag_tables()
    product = stiff_scale * conduct * jnp.asarray(
        stiff_part, conduct.dtype
    ) + mass_scale * jnp.asarray(mass_part, conduct.dtype)
    return gather_elements(product, False)


def coarse_conduct(conduct):
    layers_z, rows_y, cols_x = conduct.shape
    shaped = conduct.reshape(layers_z // 2, 2, rows_y // 2, 2, cols_x // 2, 2)
    return jnp.sum(shaped, axis=(1, 3, 5)) * 0.125


def prolong_axis(coarse, which_axis):
    pieces = node_slices(coarse, which_axis, False)
    fine_parts = [
        pieces[0],
        0.375 * pieces[0] + 0.75 * pieces[1] - 0.125 * pieces[2],
        pieces[1],
        -0.125 * pieces[0] + 0.75 * pieces[1] + 0.375 * pieces[2],
    ]
    woven_nodes = jnp.stack(fine_parts, axis=which_axis + 1)
    node_shape = list(pieces[0].shape)
    node_shape[which_axis] = 4 * pieces[0].shape[which_axis]
    woven_nodes = woven_nodes.reshape(node_shape)
    length_here = coarse.shape[which_axis]
    tail_node = lax.slice_in_dim(coarse, length_here - 1, length_here, axis=which_axis)
    return jnp.concatenate([woven_nodes, tail_node], axis=which_axis)


def prolong_all(coarse):
    result = prolong_axis(coarse, 0)
    result = prolong_axis(result, 1)
    return prolong_axis(result, 2)


def restrict_axis(fine, which_axis):
    length_here = fine.shape[which_axis]
    elements = (length_here - 1) // 4
    quarters = [
        lax.slice_in_dim(fine, q, q + 4 * elements - 3, 4, axis=which_axis) for q in range(4)
    ]
    coarse_parts = [
        quarters[0] + 0.375 * quarters[1] - 0.125 * quarters[3],
        0.75 * quarters[1] + quarters[2] + 0.75 * quarters[3],
        -0.125 * quarters[1] + 0.375 * quarters[3],
    ]
    folded = fold_back(jnp.stack(coarse_parts, 0), which_axis + 1, False)
    tail_node = lax.slice_in_dim(fine, length_here - 1, length_here, axis=which_axis)
    return folded + pad_axis(tail_node, which_axis, 2 * elements, 0)


def restrict_all(fine):
    result = restrict_axis(fine, 0)
    result = restrict_axis(result, 1)
    return restrict_axis(result, 2)


def chebyshev(right_side, diagonal, operate, degree):
    centre = 0.5 * (upper_bound + lower_bound)
    half_width = 0.5 * (upper_bound - lower_bound)
    sharpness = centre / half_width
    factor = 1.0 / sharpness
    scaled = 1.0 / diagonal
    update = scaled * right_side * (1.0 / centre)
    solution = update
    for k in range(1, degree):
        residual = right_side - operate(solution)
        next_factor = 1.0 / (2.0 * sharpness - factor)
        update = next_factor * factor * update + 2.0 * next_factor / half_width * (
            scaled * residual
        )
        solution = solution + update
        factor = next_factor
    return solution


def merge_rims(extended, which_axis):
    length_here = extended.shape[which_axis]
    inner_part = lax.slice_in_dim(extended, 1, length_here - 1, axis=which_axis)
    below_rim = lax.slice_in_dim(extended, 0, 1, axis=which_axis)
    above_rim = lax.slice_in_dim(extended, length_here - 1, length_here, axis=which_axis)
    return (
        inner_part
        + pad_axis(below_rim, which_axis, 0, length_here - 3)
        + pad_axis(above_rim, which_axis, length_here - 3, 0)
    )


def merge_all(extended, axes_list):
    for which_axis in axes_list:
        extended = merge_rims(extended, which_axis)
    return extended


def faces_fine(stacked):
    extended = padded(stacked, (("gx", 3), ("gy", 2), ("gz", 1)), 1)
    return merge_all(extended, (1, 2, 3))


def band_sums(stacked):
    extended = padded(stacked, (("gy", 2), ("gz", 1)), 1)
    return merge_all(extended, (1, 2))


def to_periodic(gathered, devices):
    layers_z, rows_y, total_x = gathered.shape
    block_x = total_x // devices
    shaped = gathered.reshape(layers_z, rows_y, devices, block_x)
    main_part = shaped[:, :, :, : block_x - 1]
    tail_part = shaped[:, :, :, block_x - 1]
    first_layer = main_part[:, :, :, :1] + jnp.roll(tail_part, 1, axis=2)[:, :, :, None]
    joined = jnp.concatenate([first_layer, main_part[:, :, :, 1:]], axis=3)
    return joined.reshape(layers_z, rows_y, devices * (block_x - 1))


def on_device(element_load, conductivity):
    load_full = pad_axis(element_load, 2, 0, 1)
    assembled = faces_fine(jnp.stack([load_full, diag_local(conductivity, 1.0, reaction_rate)], 0))
    right_side = assembled[0]
    diagonal = assembled[1]

    def operate_fine(node_field):
        return faces_fine(apply_local(node_field, conductivity, 1.0, reaction_rate, False)[None])[0]

    smooth = chebyshev(right_side, diagonal, operate_fine, DEG1)
    partial_value = load_full - apply_local(smooth, conductivity, 1.0, reaction_rate, False)
    coarse_load = restrict_all(partial_value)
    coarse_cond = coarse_conduct(conductivity)
    coarse_mass = 8.0 * reaction_rate
    coarse_diag = diag_local(coarse_cond, 2.0, coarse_mass)
    gathered = (
        lax.all_gather(coarse_load, "gx", axis=2, tiled=True),
        lax.all_gather(coarse_diag, "gx", axis=2, tiled=True),
        lax.all_gather(coarse_cond, "gx", axis=2, tiled=True),
    )
    devices_x = lax.axis_size("gx")
    right_full = to_periodic(gathered[0], devices_x)
    diag_full = to_periodic(gathered[1], devices_x)
    band_both = band_sums(jnp.stack([right_full, diag_full], 0))

    def operate_band(node_field):
        return band_sums(apply_local(node_field, gathered[2], 2.0, coarse_mass, True)[None])[0]

    full_correction = chebyshev(band_both[0], band_both[1], operate_band, DEG2)
    own_nodes = coarse_load.shape[2]
    extended = jnp.concatenate([full_correction, full_correction[:, :, :1]], axis=2)
    correction = lax.dynamic_slice_in_dim(
        extended, lax.axis_index("gx") * (own_nodes - 1), own_nodes, axis=2
    )
    corrected = smooth + prolong_all(correction)
    return corrected[:, :, : corrected.shape[2] - 1]


def solution(mesh):
    in_specs = (P("gz", "gy", "gx"), P("gz", "gy", "gx"))
    out_specs = P("gz", "gy", "gx")
    return jax.shard_map(
        on_device, mesh=mesh, in_specs=in_specs, out_specs=out_specs, check_vma=False
    )
```

profile of v0, /device:TPU:0, one launch (start us, length us, event | category | flops | bytes accessed | tf_op | source)
XLA Modules:
  0.0 134.0 jit_solution(7318380559509319765)
XLA Ops:
  0.0 0.8 multiply_add_fusion.1
  1.1 0.6 copy.792
  3.1 3.0 %collective-permute-start.1 = (f32[2,5,17,1]{3,0,2,1:T(2,128)S(1)}, f32[2,5,17,1]{3,0,2,1:T(2,128)S(1)}, u32[]{:S(2)}, u32[]{:S(2)}) collective-permute-start(f32[2,5,17,1]{3,0,2,1:T(2,128)S(1)} %get-tuple-element.142), channel_id=1, source_target_pairs={{16,0},{0,16},{17,1},{1,17},{18,2},{2,18},{19,3},{3,19},{20,4},{4,... | collective-permute-start | bytes 2048 | tf_op jit(solution)/shard_map/ppermute | solution.py:35
  7.7 1.4 %collective-permute-done.1 = f32[2,5,17,1]{3,0,2,1:T(2,128)S(1)} collective-permute-done((f32[2,5,17,1]{3,0,2,1:T(2,128)S(1)}, f32[2,5,17,1]{3,0,2,1:T(2,128)S(1)}, u32[]{:S(2)}, u32[]{:S(2)}) %collective-permute-start.1) | collective-permute-done | bytes 712 | tf_op jit(solution)/shard_map/ppermute | solution.py:35
  9.1 1.5 %collective-permute-done = f32[2,5,17,1]{3,0,2,1:T(2,128)S(1)} collective-permute-done((f32[2,5,17,1]{3,0,2,1:T(2,128)S(1)}, f32[2,5,17,1]{3,0,2,1:T(2,128)S(1)}, u32[]{:S(2)}, u32[]{:S(2)}) %collective-permute-start) | collective-permute-done | bytes 712 | tf_op jit(solution)/shard_map/ppermute | solution.py:33
  10.7 0.8 collective-permute-start.3
  11.5 1.4 %collective-permute-done.3 = f32[2,5,1,131]{3,0,2,1:T(2,128)S(1)} collective-permute-done((f32[2,5,1,131]{3,0,2,1:T(2,128)S(1)}, f32[2,5,1,131]{3,0,2,1:T(2,128)S(1)}, u32[]{:S(2)}, u32[]{:S(2)}) %collective-permute-start.3) | collective-permute-done | bytes 5272 | tf_op jit(solution)/shard_map/ppermute | solution.py:35
  12.9 1.7 %collective-permute-done.2 = f32[2,5,1,131]{3,0,2,1:T(2,128)S(1)} collective-permute-done((f32[2,5,1,131]{3,0,2,1:T(2,128)S(1)}, f32[2,5,1,131]{3,0,2,1:T(2,128)S(1)}, u32[]{:S(2)}, u32[]{:S(2)}) %collective-permute-start.2) | collective-permute-done | bytes 5272 | tf_op jit(solution)/shard_map/ppermute | solution.py:33
  14.6 0.5 pad_maximum_fusion.25
  15.1 3.7 %collective-permute-start.5 = (f32[2,1,19,131]{3,0,2,1:T(2,128)S(1)}, f32[2,1,19,131]{3,0,2,1:T(2,128)S(1)}, u32[]{:S(2)}, u32[]{:S(2)}) collective-permute-start(f32[2,1,19,131]{3,0,2,1:T(2,128)S(1)} %get-tuple-element.105), channel_id=1, source_target_pairs={{1,0},{2,1},{3,2},{0,3},{5,4},{6,5},{7,6},{4,7},{9,8},{10,9},{11,1... | collective-permute-start | bytes 59744 | tf_op jit(solution)/shard_map/ppermute | solution.py:35
  18.8 1.6 %collective-permute-done.5 = f32[2,1,19,131]{3,0,2,1:T(2,128)S(1)} collective-permute-done((f32[2,1,19,131]{3,0,2,1:T(2,128)S(1)}, f32[2,1,19,131]{3,0,2,1:T(2,128)S(1)}, u32[]{:S(2)}, u32[]{:S(2)}) %collective-permute-start.5) | collective-permute-done | bytes 19944 | tf_op jit(solution)/shard_map/ppermute | solution.py:35
  20.5 4.1 %collective-permute-done.4 = f32[2,1,19,131]{3,0,2,1:T(2,128)S(1)} collective-permute-done((f32[2,1,19,131]{3,0,2,1:T(2,128)S(1)}, f32[2,1,19,131]{3,0,2,1:T(2,128)S(1)}, u32[]{:S(2)}, u32[]{:S(2)}) %collective-permute-start.4) | collective-permute-done | bytes 19944 | tf_op jit(solution)/shard_map/ppermute | solution.py:33
  24.6 0.5 pad_add_fusion.3
  25.9 0.8 slice.1306
  26.7 0.8 slice.1305
  27.5 0.8 slice.1304
  29.7 0.6 copy.814
  31.0 1.2 collective-permute-start.7
  32.2 0.9 collective-permute-start.6
  33.4 1.9 %collective-permute-done.7 = f32[1,5,17,1]{3,2,1,0:T(8,128)S(1)} collective-permute-done((f32[1,5,17,1]{3,2,1,0:T(8,128)S(1)}, f32[1,5,17,1]{3,2,1,0:T(8,128)S(1)}, u32[]{:S(2)}, u32[]{:S(2)}) %collective-permute-start.7) | collective-permute-done | bytes 372 | tf_op jit(solution)/shard_map/ppermute | solution.py:35
  35.4 1.0 collective-permute-done.6
  37.1 7.0 %all_gather.10 = f32[3,9,130]{1,0,2:T(4,128)S(1)} all-gather(f32[3,9,65]{1,0,2:T(4,128)S(1)} %copy.888), channel_id=1, replica_groups=mesh['gx'=2,'gy'=4,'gz'=4] {'gx'}, dimensions={2}, use_global_device_ids=true | all-gather | bytes 21060 | tf_op jit(solution)/shard_map/all_gather | solution.py:261
  44.6 2.0 %collective-permute-start.10 = (f32[1,1,19,131]{3,2,1,0:T(8,128)S(1)}, f32[1,1,19,131]{3,2,1,0:T(8,128)S(1)}, u32[]{:S(2)}, u32[]{:S(2)}) collective-permute-start(f32[1,1,19,131]{3,2,1,0:T(8,128)S(1)} %copy.1043), channel_id=1, source_target_pairs={{0,1},{1,2},{2,3},{3,0},{4,5},{5,6},{6,7},{7,4},{8,9},{9,10},{10,1... | collective-permute-start | bytes 29876 | tf_op jit(solution)/shard_map/ppermute | solution.py:33
  46.6 1.8 %collective-permute-done.11 = f32[1,1,19,131]{3,2,1,0:T(8,128)S(1)} collective-permute-done((f32[1,1,19,131]{3,2,1,0:T(8,128)S(1)}, f32[1,1,19,131]{3,2,1,0:T(8,128)S(1)}, u32[]{:S(2)}, u32[]{:S(2)}) %collective-permute-start.11) | collective-permute-done | bytes 9988 | tf_op jit(solution)/shard_map/ppermute | solution.py:35
  48.4 2.1 %collective-permute-done.10 = f32[1,1,19,131]{3,2,1,0:T(8,128)S(1)} collective-permute-done((f32[1,1,19,131]{3,2,1,0:T(8,128)S(1)}, f32[1,1,19,131]{3,2,1,0:T(8,128)S(1)}, u32[]{:S(2)}, u32[]{:S(2)}) %collective-permute-start.10) | collective-permute-done | bytes 9988 | tf_op jit(solution)/shard_map/ppermute | solution.py:33
  50.8 0.8 slice.1360
  51.6 0.8 slice.1359
  52.4 0.8 slice.1358
  54.6 0.6 copy.839
  55.9 1.0 collective-permute-start.13
  56.9 1.1 collective-permute-start.12
  58.1 2.1 %collective-permute-done.13 = f32[1,5,17,1]{3,2,1,0:T(8,128)S(1)} collective-permute-done((f32[1,5,17,1]{3,2,1,0:T(8,128)S(1)}, f32[1,5,17,1]{3,2,1,0:T(8,128)S(1)}, u32[]{:S(2)}, u32[]{:S(2)}) %collective-permute-start.13) | collective-permute-done | bytes 372 | tf_op jit(solution)/shard_map/ppermute | solution.py:35
  60.3 0.9 collective-permute-done.12
  62.7 1.8 %collective-permute-done.14 = f32[1,5,1,131]{3,0,2,1:T(1,128)S(1)} collective-permute-done((f32[1,5,1,131]{3,0,2,1:T(1,128)S(1)}, f32[1,5,1,131]{3,0,2,1:T(1,128)S(1)}, u32[]{:S(2)}, u32[]{:S(2)}) %collective-permute-start.14) | collective-permute-done | bytes 2652 | tf_op jit(solution)/shard_map/ppermute | solution.py:33
  64.9 2.0 %collective-permute-start.16 = (f32[1,1,19,131]{3,2,1,0:T(8,128)S(1)}, f32[1,1,19,131]{3,2,1,0:T(8,128)S(1)}, u32[]{:S(2)}, u32[]{:S(2)}) collective-permute-start(f32[1,1,19,131]{3,2,1,0:T(8,128)S(1)} %copy.1045), channel_id=1, source_target_pairs={{0,1},{1,2},{2,3},{3,0},{4,5},{5,6},{6,7},{7,4},{8,9},{9,10},{10,1... | collective-permute-start | bytes 29876 | tf_op jit(solution)/shard_map/ppermute | solution.py:33
  67.1 1.8 %collective-permute-done.17 = f32[1,1,19,131]{3,2,1,0:T(8,128)S(1)} collective-permute-done((f32[1,1,19,131]{3,2,1,0:T(8,128)S(1)}, f32[1,1,19,131]{3,2,1,0:T(8,128)S(1)}, u32[]{:S(2)}, u32[]{:S(2)}) %collective-permute-start.17) | collective-permute-done | bytes 9988 | tf_op jit(solution)/shard_map/ppermute | solution.py:35
  69.0 1.6 %collective-permute-done.16 = f32[1,1,19,131]{3,2,1,0:T(8,128)S(1)} collective-permute-done((f32[1,1,19,131]{3,2,1,0:T(8,128)S(1)}, f32[1,1,19,131]{3,2,1,0:T(8,128)S(1)}, u32[]{:S(2)}, u32[]{:S(2)}) %collective-permute-start.16) | collective-permute-done | bytes 9988 | tf_op jit(solution)/shard_map/ppermute | solution.py:33
  70.9 0.8 slice.1414
  71.8 0.8 slice.1413
  72.6 0.8 slice.1412
  74.7 0.6 copy.864
  78.2 5.7 %all_gather.9 = f32[3,9,130]{1,0,2:T(4,128)S(1)} all-gather(f32[3,9,65]{1,0,2:T(4,128)S(1)} %copy.875), channel_id=1, replica_groups=mesh['gx'=2,'gy'=4,'gz'=4] {'gx'}, dimensions={2}, use_global_device_ids=true | all-gather | bytes 21060 | tf_op jit(solution)/shard_map/all_gather | solution.py:260
  84.7 0.5 collective-permute-start.18
  85.2 4.3 %all-gather.1 = f32[2,32,4]{1,2,0:T(4,128)S(1)} all-gather(f32[1,32,4]{1,2,0:T(4,128)S(1)} %get-tuple-element.346), channel_id=2, replica_groups=mesh['gx'=2,'gy'=4,'gz'=4] {'gx'}, dimensions={0}, use_global_device_ids=true | all-gather | bytes 1536 | tf_op jit(solution)/shard_map/all_gather | solution.py:262
  89.8 1.9 %collective-permute-start.20 = (f32[2,1,11,128]{3,1,2,0:T(1,128)S(1)}, f32[2,1,11,128]{3,1,2,0:T(1,128)S(1)}, u32[]{:S(2)}, u32[]{:S(2)}) collective-permute-start(f32[2,1,11,128]{3,1,2,0:T(1,128)S(1)} %copy.1047), channel_id=1, source_target_pairs={{0,1},{1,2},{2,3},{3,0},{4,5},{5,6},{6,7},{7,4},{8,9},{9,10},{10,1... | collective-permute-start | bytes 33800 | tf_op jit(solution)/shard_map/ppermute | solution.py:33
  91.9 1.5 %collective-permute-done.21 = f32[2,1,11,128]{3,1,2,0:T(1,128)S(1)} collective-permute-done((f32[2,1,11,128]{3,1,2,0:T(1,128)S(1)}, f32[2,1,11,128]{3,1,2,0:T(1,128)S(1)}, u32[]{:S(2)}, u32[]{:S(2)}) %collective-permute-start.21) | collective-permute-done | bytes 11296 | tf_op jit(solution)/shard_map/ppermute | solution.py:35
  93.4 2.0 %collective-permute-done.20 = f32[2,1,11,128]{3,1,2,0:T(1,128)S(1)} collective-permute-done((f32[2,1,11,128]{3,1,2,0:T(1,128)S(1)}, f32[2,1,11,128]{3,1,2,0:T(1,128)S(1)}, u32[]{:S(2)}, u32[]{:S(2)}) %collective-permute-start.20) | collective-permute-done | bytes 11296 | tf_op jit(solution)/shard_map/ppermute | solution.py:33
  99.1 0.8 collective-permute-done.23
  99.9 1.8 %collective-permute-done.22 = f32[1,3,1,128]{3,1,2,0:T(4,128)S(1)} collective-permute-done((f32[1,3,1,128]{3,1,2,0:T(4,128)S(1)}, f32[1,3,1,128]{3,1,2,0:T(4,128)S(1)}, u32[]{:S(2)}, u32[]{:S(2)}) %collective-permute-start.22) | collective-permute-done | bytes 1568 | tf_op jit(solution)/shard_map/ppermute | solution.py:33
  101.7 2.0 %collective-permute-start.24 = (f32[1,1,11,128]{3,1,2,0:T(1,128)S(1)}, f32[1,1,11,128]{3,1,2,0:T(1,128)S(1)}, u32[]{:S(2)}, u32[]{:S(2)}) collective-permute-start(f32[1,1,11,128]{3,1,2,0:T(1,128)S(1)} %get-tuple-element.315), channel_id=1, source_target_pairs={{0,1},{1,2},{2,3},{3,0},{4,5},{5,6},{6,7},{7,4},{8,9},{9,10},{10,1... | collective-permute-start | bytes 16904 | tf_op jit(solution)/shard_map/ppermute | solution.py:33
  103.7 1.6 %collective-permute-done.25 = f32[1,1,11,128]{3,1,2,0:T(1,128)S(1)} collective-permute-done((f32[1,1,11,128]{3,1,2,0:T(1,128)S(1)}, f32[1,1,11,128]{3,1,2,0:T(1,128)S(1)}, u32[]{:S(2)}, u32[]{:S(2)}) %collective-permute-start.25) | collective-permute-done | bytes 5664 | tf_op jit(solution)/shard_map/ppermute | solution.py:35
  105.3 1.9 %collective-permute-done.24 = f32[1,1,11,128]{3,1,2,0:T(1,128)S(1)} collective-permute-done((f32[1,1,11,128]{3,1,2,0:T(1,128)S(1)}, f32[1,1,11,128]{3,1,2,0:T(1,128)S(1)}, u32[]{:S(2)}, u32[]{:S(2)}) %collective-permute-start.24) | collective-permute-done | bytes 5664 | tf_op jit(solution)/shard_map/ppermute | solution.py:33
  110.9 0.8 collective-permute-done.27
  111.7 1.8 %collective-permute-done.26 = f32[1,3,1,128]{3,1,2,0:T(4,128)S(1)} collective-permute-done((f32[1,3,1,128]{3,1,2,0:T(4,128)S(1)}, f32[1,3,1,128]{3,1,2,0:T(4,128)S(1)}, u32[]{:S(2)}, u32[]{:S(2)}) %collective-permute-start.26) | collective-permute-done | bytes 1568 | tf_op jit(solution)/shard_map/ppermute | solution.py:33
  113.7 2.0 %collective-permute-start.28 = (f32[1,1,11,128]{3,1,2,0:T(1,128)S(1)}, f32[1,1,11,128]{3,1,2,0:T(1,128)S(1)}, u32[]{:S(2)}, u32[]{:S(2)}) collective-permute-start(f32[1,1,11,128]{3,1,2,0:T(1,128)S(1)} %get-tuple-element.313), channel_id=1, source_target_pairs={{0,1},{1,2},{2,3},{3,0},{4,5},{5,6},{6,7},{7,4},{8,9},{9,10},{10,1... | collective-permute-start | bytes 16904 | tf_op jit(solution)/shard_map/ppermute | solution.py:33
  115.7 1.6 %collective-permute-done.29 = f32[1,1,11,128]{3,1,2,0:T(1,128)S(1)} collective-permute-done((f32[1,1,11,128]{3,1,2,0:T(1,128)S(1)}, f32[1,1,11,128]{3,1,2,0:T(1,128)S(1)}, u32[]{:S(2)}, u32[]{:S(2)}) %collective-permute-start.29) | collective-permute-done | bytes 5664 | tf_op jit(solution)/shard_map/ppermute | solution.py:35
  117.3 1.9 %collective-permute-done.28 = f32[1,1,11,128]{3,1,2,0:T(1,128)S(1)} collective-permute-done((f32[1,1,11,128]{3,1,2,0:T(1,128)S(1)}, f32[1,1,11,128]{3,1,2,0:T(1,128)S(1)}, u32[]{:S(2)}, u32[]{:S(2)}) %collective-permute-start.28) | collective-permute-done | bytes 5664 | tf_op jit(solution)/shard_map/ppermute | solution.py:33
  122.4 0.5 collective-permute-start.30
  122.9 0.8 collective-permute-done.31
  123.7 1.8 %collective-permute-done.30 = f32[1,3,1,128]{3,1,2,0:T(4,128)S(1)} collective-permute-done((f32[1,3,1,128]{3,1,2,0:T(4,128)S(1)}, f32[1,3,1,128]{3,1,2,0:T(4,128)S(1)}, u32[]{:S(2)}, u32[]{:S(2)}) %collective-permute-start.30) | collective-permute-done | bytes 1568 | tf_op jit(solution)/shard_map/ppermute | solution.py:33
  125.5 2.0 %collective-permute-start.32 = (f32[1,1,11,128]{3,1,2,0:T(1,128)S(1)}, f32[1,1,11,128]{3,1,2,0:T(1,128)S(1)}, u32[]{:S(2)}, u32[]{:S(2)}) collective-permute-start(f32[1,1,11,128]{3,1,2,0:T(1,128)S(1)} %get-tuple-element.311), channel_id=1, source_target_pairs={{0,1},{1,2},{2,3},{3,0},{4,5},{5,6},{6,7},{7,4},{8,9},{9,10},{10,1... | collective-permute-start | bytes 16904 | tf_op jit(solution)/shard_map/ppermute | solution.py:33
  127.5 1.6 %collective-permute-done.33 = f32[1,1,11,128]{3,1,2,0:T(1,128)S(1)} collective-permute-done((f32[1,1,11,128]{3,1,2,0:T(1,128)S(1)}, f32[1,1,11,128]{3,1,2,0:T(1,128)S(1)}, u32[]{:S(2)}, u32[]{:S(2)}) %collective-permute-start.33) | collective-permute-done | bytes 5664 | tf_op jit(solution)/shard_map/ppermute | solution.py:35
  129.1 1.9 %collective-permute-done.32 = f32[1,1,11,128]{3,1,2,0:T(1,128)S(1)} collective-permute-done((f32[1,1,11,128]{3,1,2,0:T(1,128)S(1)}, f32[1,1,11,128]{3,1,2,0:T(1,128)S(1)}, u32[]{:S(2)}, u32[]{:S(2)}) %collective-permute-start.32) | collective-permute-done | bytes 5664 | tf_op jit(solution)/shard_map/ppermute | solution.py:33
  133.4 0.7 slice_add_fusion
  (479 shorter events, 28.8 us)
Async XLA Ops:
  1.7 0.8 copy-start.1
  2.2 4.0 %copy-start = (f32[2,8,64]{2,1,0:T(8,128)S(1)}, f32[2,8,64]{2,1,0:T(8,128)}, u32[]{:S(2)}) copy-start(f32[2,8,64]{2,1,0:T(8,128)} %param.7) | copy-start | bytes 12292
  2.2 4.3 %copy-start.2 = (f32[3,3,3]{2,1,0:T(4,128)S(1)}, f32[3,3,3]{2,1,0:T(4,128)}, u32[]{:S(2)}) copy-start(f32[3,3,3]{2,1,0:T(4,128)} %constant.276) | copy-start | bytes 328
  2.2 4.3 %copy-start.4 = (f32[3,3,3]{2,1,0:T(4,128)S(1)}, f32[3,3,3]{2,1,0:T(4,128)}, u32[]{:S(2)}) copy-start(f32[3,3,3]{2,1,0:T(4,128)} %constant.280) | copy-start | bytes 328
  3.1 6.0 %collective-permute-start.1 = (f32[2,5,17,1]{3,0,2,1:T(2,128)S(1)}, f32[2,5,17,1]{3,0,2,1:T(2,128)S(1)}, u32[]{:S(2)}, u32[]{:S(2)}) collective-permute-start(f32[2,5,17,1]{3,0,2,1:T(2,128)S(1)} %get-tuple-element.142), channel_id=1, source_target_pairs={{16,0},{0,16},{17,1},{1,17},{18,2},{2,18},{19,3},{3,19},{20,4},{4,... | collective-permute-start | bytes 2048 | tf_op jit(solution)/shard_map/ppermute | solution.py:35
  6.1 4.5 %collective-permute-start = (f32[2,5,17,1]{3,0,2,1:T(2,128)S(1)}, f32[2,5,17,1]{3,0,2,1:T(2,128)S(1)}, u32[]{:S(2)}, u32[]{:S(2)}) collective-permute-start(f32[2,5,17,1]{3,0,2,1:T(2,128)S(1)} %get-tuple-element.141), channel_id=1, source_target_pairs={{0,16},{16,0},{1,17},{17,1},{2,18},{18,2},{3,19},{19,3},{4,20},{20... | collective-permute-start | bytes 2048 | tf_op jit(solution)/shard_map/ppermute | solution.py:33
  7.5 17.6 %copy-start.6 = (pred[17]{0:T(512)(128)(4,1)S(1)}, pred[17]{0:T(512)(128)(4,1)}, u32[]{:S(2)}) copy-start(pred[17]{0:T(512)(128)(4,1)} %constant.38.clone.1) | copy-start | bytes 55
  7.7 17.8 %copy-start.5 = (pred[129]{0:T(512)(128)(4,1)S(1)}, pred[129]{0:T(512)(128)(4,1)}, u32[]{:S(2)}) copy-start(pred[129]{0:T(512)(128)(4,1)} %constant.39.clone.1) | copy-start | bytes 391
  10.7 2.2 %collective-permute-start.3 = (f32[2,5,1,131]{3,0,2,1:T(2,128)S(1)}, f32[2,5,1,131]{3,0,2,1:T(2,128)S(1)}, u32[]{:S(2)}, u32[]{:S(2)}) collective-permute-start(f32[2,5,1,131]{3,0,2,1:T(2,128)S(1)} %get-tuple-element.13), channel_id=1, source_target_pairs={{4,0},{8,4},{12,8},{0,12},{5,1},{9,5},{13,9},{1,13},{6,2},{10,6},{... | collective-permute-start | bytes 15728 | tf_op jit(solution)/shard_map/ppermute | solution.py:35
  11.5 3.1 %collective-permute-start.2 = (f32[2,5,1,131]{3,0,2,1:T(2,128)S(1)}, f32[2,5,1,131]{3,0,2,1:T(2,128)S(1)}, u32[]{:S(2)}, u32[]{:S(2)}) collective-permute-start(f32[2,5,1,131]{3,0,2,1:T(2,128)S(1)} %get-tuple-element.12), channel_id=1, source_target_pairs={{0,4},{4,8},{8,12},{12,0},{1,5},{5,9},{9,13},{13,1},{2,6},{6,10},{... | collective-permute-start | bytes 15728 | tf_op jit(solution)/shard_map/ppermute | solution.py:33
  15.1 5.3 %collective-permute-start.5 = (f32[2,1,19,131]{3,0,2,1:T(2,128)S(1)}, f32[2,1,19,131]{3,0,2,1:T(2,128)S(1)}, u32[]{:S(2)}, u32[]{:S(2)}) collective-permute-start(f32[2,1,19,131]{3,0,2,1:T(2,128)S(1)} %get-tuple-element.105), channel_id=1, source_target_pairs={{1,0},{2,1},{3,2},{0,3},{5,4},{6,5},{7,6},{4,7},{9,8},{10,9},{11,1... | collective-permute-start | bytes 59744 | tf_op jit(solution)/shard_map/ppermute | solution.py:35
  18.8 5.8 %collective-permute-start.4 = (f32[2,1,19,131]{3,0,2,1:T(2,128)S(1)}, f32[2,1,19,131]{3,0,2,1:T(2,128)S(1)}, u32[]{:S(2)}, u32[]{:S(2)}) collective-permute-start(f32[2,1,19,131]{3,0,2,1:T(2,128)S(1)} %get-tuple-element.104), channel_id=1, source_target_pairs={{0,1},{1,2},{2,3},{3,0},{4,5},{5,6},{6,7},{7,4},{8,9},{9,10},{10,1... | collective-permute-start | bytes 59744 | tf_op jit(solution)/shard_map/ppermute | solution.py:33
  31.0 4.3 %collective-permute-start.7 = (f32[1,5,17,1]{3,2,1,0:T(8,128)S(1)}, f32[1,5,17,1]{3,2,1,0:T(8,128)S(1)}, u32[]{:S(2)}, u32[]{:S(2)}) collective-permute-start(f32[1,5,17,1]{3,2,1,0:T(8,128)S(1)} %get-tuple-element.162), channel_id=1, source_target_pairs={{16,0},{0,16},{17,1},{1,17},{18,2},{2,18},{19,3},{3,19},{20,4},{4,... | collective-permute-start | bytes 1028 | tf_op jit(solution)/shard_map/ppermute | solution.py:35
  32.2 4.2 %collective-permute-start.6 = (f32[1,5,17,1]{3,2,1,0:T(8,128)S(1)}, f32[1,5,17,1]{3,2,1,0:T(8,128)S(1)}, u32[]{:S(2)}, u32[]{:S(2)}) collective-permute-start(f32[1,5,17,1]{3,2,1,0:T(8,128)S(1)} %get-tuple-element.161), channel_id=1, source_target_pairs={{0,16},{16,0},{1,17},{17,1},{2,18},{18,2},{3,19},{19,3},{4,20},{20... | collective-permute-start | bytes 1028 | tf_op jit(solution)/shard_map/ppermute | solution.py:33
  36.6 7.5 %collective-permute-start.9 = (f32[1,5,1,131]{3,0,2,1:T(1,128)S(1)}, f32[1,5,1,131]{3,0,2,1:T(1,128)S(1)}, u32[]{:S(2)}, u32[]{:S(2)}) collective-permute-start(f32[1,5,1,131]{3,0,2,1:T(1,128)S(1)} %get-tuple-element.135), channel_id=1, source_target_pairs={{4,0},{8,4},{12,8},{0,12},{5,1},{9,5},{13,9},{1,13},{6,2},{10,6},{... | collective-permute-start | bytes 7868 | tf_op jit(solution)/shard_map/ppermute | solution.py:35
  36.6 7.5 %collective-permute-start.8 = (f32[1,5,1,131]{3,0,2,1:T(1,128)S(1)}, f32[1,5,1,131]{3,0,2,1:T(1,128)S(1)}, u32[]{:S(2)}, u32[]{:S(2)}) collective-permute-start(f32[1,5,1,131]{3,0,2,1:T(1,128)S(1)} %get-tuple-element.134), channel_id=1, source_target_pairs={{0,4},{4,8},{8,12},{12,0},{1,5},{5,9},{9,13},{13,1},{2,6},{6,10},{... | collective-permute-start | bytes 7868 | tf_op jit(solution)/shard_map/ppermute | solution.py:33
  44.5 3.9 %collective-permute-start.11 = (f32[1,1,19,131]{3,2,1,0:T(8,128)S(1)}, f32[1,1,19,131]{3,2,1,0:T(8,128)S(1)}, u32[]{:S(2)}, u32[]{:S(2)}) collective-permute-start(f32[1,1,19,131]{3,2,1,0:T(8,128)S(1)} %copy.1042), channel_id=1, source_target_pairs={{1,0},{2,1},{3,2},{0,3},{5,4},{6,5},{7,6},{4,7},{9,8},{10,9},{11,1... | collective-permute-start | bytes 29876 | tf_op jit(solution)/shard_map/ppermute | solution.py:35
  44.6 5.9 %collective-permute-start.10 = (f32[1,1,19,131]{3,2,1,0:T(8,128)S(1)}, f32[1,1,19,131]{3,2,1,0:T(8,128)S(1)}, u32[]{:S(2)}, u32[]{:S(2)}) collective-permute-start(f32[1,1,19,131]{3,2,1,0:T(8,128)S(1)} %copy.1043), channel_id=1, source_target_pairs={{0,1},{1,2},{2,3},{3,0},{4,5},{5,6},{6,7},{7,4},{8,9},{9,10},{10,1... | collective-permute-start | bytes 29876 | tf_op jit(solution)/shard_map/ppermute | solution.py:33
  55.9 4.3 %collective-permute-start.13 = (f32[1,5,17,1]{3,2,1,0:T(8,128)S(1)}, f32[1,5,17,1]{3,2,1,0:T(8,128)S(1)}, u32[]{:S(2)}, u32[]{:S(2)}) collective-permute-start(f32[1,5,17,1]{3,2,1,0:T(8,128)S(1)} %get-tuple-element.160), channel_id=1, source_target_pairs={{16,0},{0,16},{17,1},{1,17},{18,2},{2,18},{19,3},{3,19},{20,4},{4,... | collective-permute-start | bytes 1028 | tf_op jit(solution)/shard_map/ppermute | solution.py:35
  56.9 4.2 %collective-permute-start.12 = (f32[1,5,17,1]{3,2,1,0:T(8,128)S(1)}, f32[1,5,17,1]{3,2,1,0:T(8,128)S(1)}, u32[]{:S(2)}, u32[]{:S(2)}) collective-permute-start(f32[1,5,17,1]{3,2,1,0:T(8,128)S(1)} %get-tuple-element.159), channel_id=1, source_target_pairs={{0,16},{16,0},{1,17},{17,1},{2,18},{18,2},{3,19},{19,3},{4,20},{20... | collective-permute-start | bytes 1028 | tf_op jit(solution)/shard_map/ppermute | solution.py:33
  61.3 1.4 %collective-permute-start.15 = (f32[1,5,1,131]{3,0,2,1:T(1,128)S(1)}, f32[1,5,1,131]{3,0,2,1:T(1,128)S(1)}, u32[]{:S(2)}, u32[]{:S(2)}) collective-permute-start(f32[1,5,1,131]{3,0,2,1:T(1,128)S(1)} %get-tuple-element.130), channel_id=1, source_target_pairs={{4,0},{8,4},{12,8},{0,12},{5,1},{9,5},{13,9},{1,13},{6,2},{10,6},{... | collective-permute-start | bytes 7868 | tf_op jit(solution)/shard_map/ppermute | solution.py:35
  61.4 3.1 %collective-permute-start.14 = (f32[1,5,1,131]{3,0,2,1:T(1,128)S(1)}, f32[1,5,1,131]{3,0,2,1:T(1,128)S(1)}, u32[]{:S(2)}, u32[]{:S(2)}) collective-permute-start(f32[1,5,1,131]{3,0,2,1:T(1,128)S(1)} %get-tuple-element.129), channel_id=1, source_target_pairs={{0,4},{4,8},{8,12},{12,0},{1,5},{5,9},{9,13},{13,1},{2,6},{6,10},{... | collective-permute-start | bytes 7868 | tf_op jit(solution)/shard_map/ppermute | solution.py:33
  64.8 4.1 %collective-permute-start.17 = (f32[1,1,19,131]{3,2,1,0:T(8,128)S(1)}, f32[1,1,19,131]{3,2,1,0:T(8,128)S(1)}, u32[]{:S(2)}, u32[]{:S(2)}) collective-permute-start(f32[1,1,19,131]{3,2,1,0:T(8,128)S(1)} %copy.1044), channel_id=1, source_target_pairs={{1,0},{2,1},{3,2},{0,3},{5,4},{6,5},{7,6},{4,7},{9,8},{10,9},{11,1... | collective-permute-start | bytes 29876 | tf_op jit(solution)/shard_map/ppermute | solution.py:35
  64.9 5.7 %collective-permute-start.16 = (f32[1,1,19,131]{3,2,1,0:T(8,128)S(1)}, f32[1,1,19,131]{3,2,1,0:T(8,128)S(1)}, u32[]{:S(2)}, u32[]{:S(2)}) collective-permute-start(f32[1,1,19,131]{3,2,1,0:T(8,128)S(1)} %copy.1045), channel_id=1, source_target_pairs={{0,1},{1,2},{2,3},{3,0},{4,5},{5,6},{6,7},{7,4},{8,9},{9,10},{10,1... | collective-permute-start | bytes 29876 | tf_op jit(solution)/shard_map/ppermute | solution.py:33
  77.8 17.6 %copy-start.3 = (pred[9]{0:T(512)(128)(4,1)S(1)}, pred[9]{0:T(512)(128)(4,1)}, u32[]{:S(2)}) copy-start(pred[9]{0:T(512)(128)(4,1)} %constant.59.clone.1) | copy-start | bytes 31
  84.7 4.9 %collective-permute-start.19 = (f32[2,3,1,128]{3,0,2,1:T(2,128)S(1)}, f32[2,3,1,128]{3,0,2,1:T(2,128)S(1)}, u32[]{:S(2)}, u32[]{:S(2)}) collective-permute-start(f32[2,3,1,128]{3,0,2,1:T(2,128)S(1)} %get-tuple-element.308), channel_id=1, source_target_pairs={{4,0},{8,4},{12,8},{0,12},{5,1},{9,5},{13,9},{1,13},{6,2},{10,6},{... | collective-permute-start | bytes 9224 | tf_op jit(solution)/shard_map/ppermute | solution.py:35
  84.7 4.8 %collective-permute-start.18 = (f32[2,3,1,128]{3,0,2,1:T(2,128)S(1)}, f32[2,3,1,128]{3,0,2,1:T(2,128)S(1)}, u32[]{:S(2)}, u32[]{:S(2)}) collective-permute-start(f32[2,3,1,128]{3,0,2,1:T(2,128)S(1)} %get-tuple-element.307), channel_id=1, source_target_pairs={{0,4},{4,8},{8,12},{12,0},{1,5},{5,9},{9,13},{13,1},{2,6},{6,10},{... | collective-permute-start | bytes 9224 | tf_op jit(solution)/shard_map/ppermute | solution.py:33
  89.6 3.7 %collective-permute-start.21 = (f32[2,1,11,128]{3,1,2,0:T(1,128)S(1)}, f32[2,1,11,128]{3,1,2,0:T(1,128)S(1)}, u32[]{:S(2)}, u32[]{:S(2)}) collective-permute-start(f32[2,1,11,128]{3,1,2,0:T(1,128)S(1)} %copy.1046), channel_id=1, source_target_pairs={{1,0},{2,1},{3,2},{0,3},{5,4},{6,5},{7,6},{4,7},{9,8},{10,9},{11,1... | collective-permute-start | bytes 33800 | tf_op jit(solution)/shard_map/ppermute | solution.py:35
  89.8 5.5 %collective-permute-start.20 = (f32[2,1,11,128]{3,1,2,0:T(1,128)S(1)}, f32[2,1,11,128]{3,1,2,0:T(1,128)S(1)}, u32[]{:S(2)}, u32[]{:S(2)}) collective-permute-start(f32[2,1,11,128]{3,1,2,0:T(1,128)S(1)} %copy.1047), channel_id=1, source_target_pairs={{0,1},{1,2},{2,3},{3,0},{4,5},{5,6},{6,7},{7,4},{8,9},{9,10},{10,1... | collective-permute-start | bytes 33800 | tf_op jit(solution)/shard_map/ppermute | solution.py:33
  98.5 1.4 %collective-permute-start.23 = (f32[1,3,1,128]{3,1,2,0:T(4,128)S(1)}, f32[1,3,1,128]{3,1,2,0:T(4,128)S(1)}, u32[]{:S(2)}, u32[]{:S(2)}) collective-permute-start(f32[1,3,1,128]{3,1,2,0:T(4,128)S(1)} %get-tuple-element.327), channel_id=1, source_target_pairs={{4,0},{8,4},{12,8},{0,12},{5,1},{9,5},{13,9},{1,13},{6,2},{10,6},{... | collective-permute-start | bytes 4616 | tf_op jit(solution)/shard_map/ppermute | solution.py:35
  98.6 3.1 %collective-permute-start.22 = (f32[1,3,1,128]{3,1,2,0:T(4,128)S(1)}, f32[1,3,1,128]{3,1,2,0:T(4,128)S(1)}, u32[]{:S(2)}, u32[]{:S(2)}) collective-permute-start(f32[1,3,1,128]{3,1,2,0:T(4,128)S(1)} %get-tuple-element.326), channel_id=1, source_target_pairs={{0,4},{4,8},{8,12},{12,0},{1,5},{5,9},{9,13},{13,1},{2,6},{6,10},{... | collective-permute-start | bytes 4616 | tf_op jit(solution)/shard_map/ppermute | solution.py:33
  101.7 3.7 %collective-permute-start.25 = (f32[1,1,11,128]{3,1,2,0:T(1,128)S(1)}, f32[1,1,11,128]{3,1,2,0:T(1,128)S(1)}, u32[]{:S(2)}, u32[]{:S(2)}) collective-permute-start(f32[1,1,11,128]{3,1,2,0:T(1,128)S(1)} %get-tuple-element.316), channel_id=1, source_target_pairs={{1,0},{2,1},{3,2},{0,3},{5,4},{6,5},{7,6},{4,7},{9,8},{10,9},{11,1... | collective-permute-start | bytes 16904 | tf_op jit(solution)/shard_map/ppermute | solution.py:35
  101.7 5.5 %collective-permute-start.24 = (f32[1,1,11,128]{3,1,2,0:T(1,128)S(1)}, f32[1,1,11,128]{3,1,2,0:T(1,128)S(1)}, u32[]{:S(2)}, u32[]{:S(2)}) collective-permute-start(f32[1,1,11,128]{3,1,2,0:T(1,128)S(1)} %get-tuple-element.315), channel_id=1, source_target_pairs={{0,1},{1,2},{2,3},{3,0},{4,5},{5,6},{6,7},{7,4},{8,9},{9,10},{10,1... | collective-permute-start | bytes 16904 | tf_op jit(solution)/shard_map/ppermute | solution.py:33
  110.3 1.4 %collective-permute-start.27 = (f32[1,3,1,128]{3,1,2,0:T(4,128)S(1)}, f32[1,3,1,128]{3,1,2,0:T(4,128)S(1)}, u32[]{:S(2)}, u32[]{:S(2)}) collective-permute-start(f32[1,3,1,128]{3,1,2,0:T(4,128)S(1)} %get-tuple-element.325), channel_id=1, source_target_pairs={{4,0},{8,4},{12,8},{0,12},{5,1},{9,5},{13,9},{1,13},{6,2},{10,6},{... | collective-permute-start | bytes 4616 | tf_op jit(solution)/shard_map/ppermute | solution.py:35
  110.4 3.1 %collective-permute-start.26 = (f32[1,3,1,128]{3,1,2,0:T(4,128)S(1)}, f32[1,3,1,128]{3,1,2,0:T(4,128)S(1)}, u32[]{:S(2)}, u32[]{:S(2)}) collective-permute-start(f32[1,3,1,128]{3,1,2,0:T(4,128)S(1)} %get-tuple-element.324), channel_id=1, source_target_pairs={{0,4},{4,8},{8,12},{12,0},{1,5},{5,9},{9,13},{13,1},{2,6},{6,10},{... | collective-permute-start | bytes 4616 | tf_op jit(solution)/shard_map/ppermute | solution.py:33
  113.4 3.9 %collective-permute-start.29 = (f32[1,1,11,128]{3,1,2,0:T(1,128)S(1)}, f32[1,1,11,128]{3,1,2,0:T(1,128)S(1)}, u32[]{:S(2)}, u32[]{:S(2)}) collective-permute-start(f32[1,1,11,128]{3,1,2,0:T(1,128)S(1)} %get-tuple-element.314), channel_id=1, source_target_pairs={{1,0},{2,1},{3,2},{0,3},{5,4},{6,5},{7,6},{4,7},{9,8},{10,9},{11,1... | collective-permute-start | bytes 16904 | tf_op jit(solution)/shard_map/ppermute | solution.py:35
  113.7 5.5 %collective-permute-start.28 = (f32[1,1,11,128]{3,1,2,0:T(1,128)S(1)}, f32[1,1,11,128]{3,1,2,0:T(1,128)S(1)}, u32[]{:S(2)}, u32[]{:S(2)}) collective-permute-start(f32[1,1,11,128]{3,1,2,0:T(1,128)S(1)} %get-tuple-element.313), channel_id=1, source_target_pairs={{0,1},{1,2},{2,3},{3,0},{4,5},{5,6},{6,7},{7,4},{8,9},{9,10},{10,1... | collective-permute-start | bytes 16904 | tf_op jit(solution)/shard_map/ppermute | solution.py:33
  122.3 1.4 %collective-permute-start.31 = (f32[1,3,1,128]{3,1,2,0:T(4,128)S(1)}, f32[1,3,1,128]{3,1,2,0:T(4,128)S(1)}, u32[]{:S(2)}, u32[]{:S(2)}) collective-permute-start(f32[1,3,1,128]{3,1,2,0:T(4,128)S(1)} %get-tuple-element.323), channel_id=1, source_target_pairs={{4,0},{8,4},{12,8},{0,12},{5,1},{9,5},{13,9},{1,13},{6,2},{10,6},{... | collective-permute-start | bytes 4616 | tf_op jit(solution)/shard_map/ppermute | solution.py:35
  122.4 3.1 %collective-permute-start.30 = (f32[1,3,1,128]{3,1,2,0:T(4,128)S(1)}, f32[1,3,1,128]{3,1,2,0:T(4,128)S(1)}, u32[]{:S(2)}, u32[]{:S(2)}) collective-permute-start(f32[1,3,1,128]{3,1,2,0:T(4,128)S(1)} %get-tuple-element.322), channel_id=1, source_target_pairs={{0,4},{4,8},{8,12},{12,0},{1,5},{5,9},{9,13},{13,1},{2,6},{6,10},{... | collective-permute-start | bytes 4616 | tf_op jit(solution)/shard_map/ppermute | solution.py:33
  125.5 3.7 %collective-permute-start.33 = (f32[1,1,11,128]{3,1,2,0:T(1,128)S(1)}, f32[1,1,11,128]{3,1,2,0:T(1,128)S(1)}, u32[]{:S(2)}, u32[]{:S(2)}) collective-permute-start(f32[1,1,11,128]{3,1,2,0:T(1,128)S(1)} %get-tuple-element.312), channel_id=1, source_target_pairs={{1,0},{2,1},{3,2},{0,3},{5,4},{6,5},{7,6},{4,7},{9,8},{10,9},{11,1... | collective-permute-start | bytes 16904 | tf_op jit(solution)/shard_map/ppermute | solution.py:35
  125.5 5.5 %collective-permute-start.32 = (f32[1,1,11,128]{3,1,2,0:T(1,128)S(1)}, f32[1,1,11,128]{3,1,2,0:T(1,128)S(1)}, u32[]{:S(2)}, u32[]{:S(2)}) collective-permute-start(f32[1,1,11,128]{3,1,2,0:T(1,128)S(1)} %get-tuple-element.311), channel_id=1, source_target_pairs={{0,1},{1,2},{2,3},{3,0},{4,5},{5,6},{6,7},{7,4},{8,9},{9,10},{10,1... | collective-permute-start | bytes 16904 | tf_op jit(solution)/shard_map/ppermute | solution.py:33
where the time goes:
time: 134 us
  waiting for transfers between devices  48.7 us (36%)
  starting transfers between devices  27.7 us (21%)
  local copies, waits for them, and re-layouts  23.7 us (18%)
  blocking collectives  17 us (13%)
  other arithmetic  14.1 us (11%)
  between operations  2.88 us (2%)
    ppermute x17, waiting for transfers between devices, padded(): lax.ppermute(tail, axis, [(i, (i + 1) % count) for i in range(count)])  27.5 us
    ppermute x17, waiting for transfers between devices, padded(): lax.ppermute(head, axis, [((i + 1) % count, i) for i in range(count)])  21.2 us
    ppermute x17, starting transfers between devices, padded(): lax.ppermute(tail, axis, [(i, (i + 1) % count) for i in range(count)])  17.1 us
    ppermute x17, starting transfers between devices, padded(): lax.ppermute(head, axis, [((i + 1) % count, i) for i in range(count)])  10.6 us
    slice x12, local copies, waits for them, and re-layouts, node_slices(): lax.slice_in_dim(node_field, a, a + 2 * elements - 1, 2, axis=which_axis)  8.73 us
    all_gather x1, blocking collectives, on_device(): lax.all_gather(coarse_diag, 'gx', axis=2, tiled=True)  6.98 us
    all_gather x1, blocking collectives, on_device(): lax.all_gather(coarse_load, 'gx', axis=2, tiled=True)  5.67 us
    all_gather x1, blocking collectives, on_device(): lax.all_gather(coarse_cond, 'gx', axis=2, tiled=True)  4.33 us
  transfers between devices with their start and end apart: 34, of which 30 were waited for; matrix products, arithmetic and copies ran while one was open for 2% of the time, Pallas kernels for 0%

commit v1 on v0

v1 whole, which is shorter than its diff:
```python
import functools

import jax
import jax.numpy as jnp
from jax import lax
from jax.experimental import pallas as pl
from jax.experimental.pallas import tpu as pltpu
from jax.sharding import PartitionSpec as P

DEG1 = 3
DEG2 = 4
REACTION = 0.05
LOWER = 0.25
UPPER = 2.5
EIG = (0.0, 12.0, 60.0)
W = (1.0 / 36.0, 1.0 / 12.0, 1.0 / 45.0)
MESH = pl.DeviceIdType.MESH
STEPS = ((1, 0), (-1, 0), (0, 1), (0, -1), (1, 1), (1, -1), (-1, 1), (-1, -1))


def iota(shape, dim):
    return lax.broadcasted_iota(jnp.int32, shape, dim)


def dot(a, b):
    return jnp.dot(a, b, precision=lax.Precision.HIGHEST, preferred_element_type=jnp.float32)


def weight(d, odd):
    a = jnp.abs(d)
    even_w = jnp.where(a == 0, 1.0, jnp.where(a == 1, 0.375, jnp.where(a == 3, -0.125, 0.0)))
    odd_w = jnp.where(a == 0, 1.0, jnp.where(a == 1, 0.75, 0.0))
    return jnp.where(odd, odd_w, even_w)


def wrapped(d, period):
    d = jnp.where(d > period // 2, d - period, d)
    return jnp.where(d < -(period // 2), d + period, d)


def x_matrices(lanes):
    n = 2 * lanes
    r, c = iota((n, n), 0), iota((n, n), 1)
    split = jnp.where(r == 2 * (c % lanes) + c // lanes, 1.0, 0.0)
    q, e = r % 128, (r // 128) * 64 + r % 128
    hit = ((c < lanes) & (e == c)) | ((c >= lanes) & (e // 2 == c % (lanes // 2)))
    place = jnp.where((q < 64) & hit, 1.0, 0.0)
    node = 2 * (r % lanes) + r // lanes
    cp, m = c // lanes, c % (lanes // 2)
    restrict = weight(wrapped(node - 4 * m - 2 * cp, n), cp == 1)
    r, c = iota((n, 128), 0), iota((n, 128), 1)
    merge = jnp.where(2 * (r % lanes) + r // lanes == c, 1.0, 0.0)
    cp, m = r // lanes, r % lanes
    prolong = jnp.where(
        m < lanes // 2, weight(wrapped(c - 4 * m - 2 * cp, n), cp == 1), 0.0
    )
    return split, place, restrict, jnp.concatenate([merge, prolong], 1)


def fine_row(r):
    kind, i = r // 8, r % 8
    return jnp.where(kind == 2, jnp.where(i == 7, 16, 1000), 2 * i + kind)


def coarse_row(r):
    kind, i = r // 8, r % 8
    low = jnp.where(i < 4, 4 * i + 2 * kind, -1000)
    return jnp.where(kind == 2, jnp.where(i == 3, 16, -1000), low), kind == 1


def y_matrices():
    r, c = iota((24, 24), 0), iota((24, 24), 1)
    at, odd = coarse_row(r)
    restrict = weight(fine_row(c) - at, odd)
    at, odd = coarse_row(c)
    prolong = weight(r - at, odd)
    merge = jnp.where(fine_row(c) == r, 1.0, 0.0)
    return restrict, jnp.concatenate([merge, prolong], 1)


def roll_x(v, step):
    lanes = v.shape[-1]
    return pltpu.roll(v.reshape(-1, lanes), step % lanes, 1).reshape(v.shape)


def roll_y(v, step):
    flat = v.reshape((-1,) + v.shape[-2:])
    return pltpu.roll(flat, step % 8, 1).reshape(v.shape)


def forward(a, b, c):
    s = a + c
    return s + 4.0 * b, a - c, s - 2.0 * b


def backward(a, b, c, squared):
    s = a + c
    if squared:
        return s + b, 16.0 * a + 4.0 * c, s + b
    return s + b, 4.0 * a - 2.0 * c, s - b


def factors(cond, h):
    cells = cond.shape[0]
    out = []
    for l in range(3):
        rows = []
        for z in range(cells):
            for j in range(3):
                for i in range(3):
                    w = W[i] * W[j] * W[l]
                    rows.append(
                        cond[z] * (w * h * (EIG[i] + EIG[j] + EIG[l])) + w * REACTION * h**3
                    )
        out.append(jnp.stack(rows, 0).reshape((cells, 3, 3) + cond.shape[1:]))
    return out


def to_nodes(modes, squared=False):
    cells = modes[0].shape[0]
    row = iota(modes[0].shape[-2:], 0)
    low, mid, up = backward(*modes, squared)
    layers = [low[0]]
    for z in range(cells):
        layers.append(mid[z])
        layers.append(up[z] + low[z + 1] if z + 1 < cells else up[z])
    q = jnp.stack(layers, 0)
    low, mid, up = backward(q[:, 0], q[:, 1], q[:, 2], squared)
    even = low + jnp.where(row == 0, 0.0, roll_y(up, 1))
    q = jnp.stack([even, mid, up], 2)
    low, mid, up = backward(q[:, 0], q[:, 1], q[:, 2], squared)
    return low + roll_x(up, 1), mid


def apply_local(field, factor, ny):
    even, odd = field
    cells = factor[0].shape[0]
    row = iota(even.shape[-2:], 0)
    g = jnp.stack(forward(even, odd, roll_x(even, -1)), 0)
    low, mid, end = g[:, :, 0], g[:, :, 1], g[:, :, 2]
    up = jnp.where(row == ny - 1, end, roll_y(low, -1))
    y = jnp.stack(forward(low, mid, up), 0)
    parts = [jnp.stack([y[:, :, 2 * z + a] for z in range(cells)], 0) for a in range(3)]
    modes = forward(*parts)
    return to_nodes([m * f for m, f in zip(modes, factor)])


def exchange(fields, phase, ny, bufs):
    zs, zr, ys, yr, cs, cr, send_sem, recv_sem = bufs
    flat = [part for field in fields for part in field]
    count = len(flat)
    layers = flat[0].shape[0]
    last = layers - 1
    row = iota(flat[0].shape[-2:], 0)
    for f, part in enumerate(flat):
        zs[phase, 0, f] = part[last]
        zs[phase, 1, f] = part[0]
        for l in range(layers):
            ys[phase, 0, f, l : l + 1] = part[l, 2, ny - 1 : ny]
            ys[phase, 1, f, l : l + 1] = part[l, 0, 0:1]
        cs[phase, 0, f : f + 1] = part[last, 2, ny - 1 : ny]
        cs[phase, 1, f : f + 1] = part[0, 2, ny - 1 : ny]
        cs[phase, 2, f : f + 1] = part[last, 0, 0:1]
        cs[phase, 3, f : f + 1] = part[0, 0, 0:1]
    gy, gz = lax.axis_size("gy"), lax.axis_size("gz")
    iy, iz = lax.axis_index("gy"), lax.axis_index("gz")
    copies = []
    for k in (2, 3, 0, 1, 4, 5, 6, 7):
        dy, dz = STEPS[k]
        if k < 2:
            src, dst = ys.at[phase, k, pl.ds(0, count)], yr.at[phase, k, pl.ds(0, count)]
        elif k < 4:
            src, dst = zs.at[phase, k - 2, pl.ds(0, count)], zr.at[phase, k - 2, pl.ds(0, count)]
        else:
            src, dst = cs.at[phase, k - 4], cr.at[phase, k - 4]
        copy = pltpu.make_async_remote_copy(
            src_ref=src,
            dst_ref=dst,
            send_sem=send_sem.at[phase, k],
            recv_sem=recv_sem.at[phase, k],
            device_id={"gy": lax.rem(iy + dy + gy, gy), "gz": lax.rem(iz + dz + gz, gz)},
            device_id_type=MESH,
        )
        copy.start()
        copies.append(copy)
    for copy in copies:
        copy.wait_recv()
    out = []
    for f, part in enumerate(flat):
        done = []
        for l in range(layers):
            first = yr[phase, 0, f, l : l + 1]
            end = yr[phase, 1, f, l : l + 1]
            if l == last:
                first = first + cr[phase, 1, f : f + 1]
                end = end + cr[phase, 3, f : f + 1]
            if l == 0:
                first = first + cr[phase, 0, f : f + 1]
                end = end + cr[phase, 2, f : f + 1]
            low = part[l, 0] + jnp.where(row == 0, first, 0.0)
            layer = jnp.stack([low, part[l, 1], part[l, 2] + end], 0)
            if l == 0:
                layer = layer + zr[phase, 0, f]
            if l == last:
                layer = layer + zr[phase, 1, f]
            done.append(layer)
        out.append(jnp.stack(done, 0))
    return [(out[2 * i], out[2 * i + 1]) for i in range(len(fields))], copies


def inverse(diagonal, ny):
    row = iota(diagonal.shape[-2:], 0)
    whole = jnp.where(row < ny, 1.0 / diagonal[:, 0:2], 0.0)
    end = jnp.where(row == ny - 1, 1.0 / diagonal[:, 2:3], 0.0)
    return jnp.concatenate([whole, end], 1)


def chebyshev(right, diagonal, factor, degree, ny, phase, bufs):
    centre = 0.5 * (UPPER + LOWER)
    half = 0.5 * (UPPER - LOWER)
    sharp = centre / half
    f = 1.0 / sharp
    scaled = [inverse(d, ny) for d in diagonal]
    update = [s * r * (1.0 / centre) for s, r in zip(scaled, right)]
    total = update
    started = []
    for k in range(1, degree):
        (image,), copies = exchange([apply_local(total, factor, ny)], phase + k - 1, ny, bufs)
        started += copies
        g = 1.0 / (2.0 * sharp - f)
        update = [
            (g * f) * u + (2.0 * g / half) * (s * (r - a))
            for u, s, r, a in zip(update, scaled, right, image)
        ]
        total = [t + u for t, u in zip(total, update)]
        f = g
    return total, started


def kernel(load_ref, cond_ref, out_ref, line, cells, cell_out, zs, zr, ys, yr, cs, cr,
           send_sem, recv_sem, x_send, x_recv):
    gx, gy, gz = lax.axis_size("gx"), lax.axis_size("gy"), lax.axis_size("gz")
    ix, iy, iz = lax.axis_index("gx"), lax.axis_index("gy"), lax.axis_index("gz")
    lanes = 64 * gx
    bufs = (zs, zr, ys, yr, cs, cr, send_sem, recv_sem)
    barrier = pltpu.get_barrier_semaphore()
    for dy, dz in STEPS:
        pl.semaphore_signal(
            barrier, inc=1,
            device_id={"gy": lax.rem(iy + dy + gy, gy), "gz": lax.rem(iz + dz + gz, gz)},
            device_id_type=MESH,
        )
    for d in range(1, gx):
        pl.semaphore_signal(
            barrier, inc=1, device_id={"gx": lax.rem(ix + d, gx)}, device_id_type=MESH
        )
    cell_out[...] = jnp.zeros(cell_out.shape, jnp.float32)
    cell_out[:, :, 0:64] = cond_ref[...]
    pl.semaphore_wait(barrier, len(STEPS) + gx - 1)
    started = []
    arrivals = []
    for d in range(1, gx):
        for k, (src, dst) in enumerate(((load_ref, line), (cell_out, cells))):
            copy = pltpu.make_async_remote_copy(
                src_ref=src,
                dst_ref=dst.at[gx - d - 1],
                send_sem=x_send.at[k, d - 1],
                recv_sem=x_recv.at[k, gx - d - 1],
                device_id={"gx": lax.rem(ix + d, gx)},
                device_id_type=MESH,
            )
            copy.start()
            arrivals.append(copy)
    split, place, restrict_x, out_x = x_matrices(lanes)
    restrict_y, out_y = y_matrices()
    for copy in arrivals:
        copy.wait_recv()
    started += arrivals

    def rows(ref):
        parts = []
        for z in range(5):
            parts.append(ref[z, pl.ds(0, 8, stride=2), :])
            parts.append(ref[z, pl.ds(1, 8, stride=2), :])
            parts.append(jnp.broadcast_to(ref[z, 16:17, :], (8, 128)))
        return jnp.concatenate(parts, 0)

    joined = jnp.concatenate(
        [rows(load_ref)] + [rows(line.at[d]) for d in range(gx - 1)], 1
    )
    loads = dot(joined, split)
    load = (loads[:, :lanes].reshape(5, 3, 8, lanes), loads[:, lanes:].reshape(5, 3, 8, lanes))
    joined = jnp.concatenate(
        [cell_out[...].reshape(16, 128)] + [cells[d].reshape(16, 128) for d in range(gx - 1)], 1
    )
    conds = dot(joined, place)
    cond = conds[:, :lanes].reshape(2, 8, lanes)
    pair = conds[:8, lanes:] + conds[8:, lanes:]
    r, c = iota((8, 8), 0), iota((8, 8), 1)
    coarse_cond = dot(jnp.where(c // 2 == r, 0.125, 0.0), pair).reshape(1, 8, lanes)

    fine = factors(cond, 1.0)
    (right, diagonal), copies = exchange([load, to_nodes(fine, True)], 0, 8, bufs)
    started += copies
    smooth, copies = chebyshev(right, diagonal, fine, DEG1, 8, 1, bufs)
    started += copies
    image = apply_local(smooth, fine, 8)
    part = [
        jnp.concatenate([(b - a).reshape(5, 24, lanes) for b, a in zip(load, image)], 2)
    ][0]
    f0, f1, f2, f3, f4 = (part[z] for z in range(5))
    three = jnp.concatenate(
        [
            f0 + 0.375 * f1 - 0.125 * f3,
            0.75 * f1 + f2 + 0.75 * f3,
            -0.125 * f1 + 0.375 * f3 + f4,
        ],
        0,
    )
    three = dot(three, restrict_x).reshape(3, 24, 2 * lanes)
    wide = dot(restrict_y, jnp.concatenate([three[z] for z in range(3)], 1))
    coarse_load = tuple(
        jnp.stack(
            [
                wide[:, (2 * z + p) * lanes : (2 * z + p + 1) * lanes].reshape(3, 8, lanes)
                for z in range(3)
            ],
            0,
        )
        for p in range(2)
    )
    coarse = factors(coarse_cond, 2.0)
    (right, diagonal), copies = exchange(
        [coarse_load, to_nodes(coarse, True)], DEG1, 4, bufs
    )
    started += copies
    correction, copies = chebyshev(right, diagonal, coarse, DEG2, 4, DEG1 + 1, bufs)
    started += copies

    own = jnp.concatenate([s.reshape(120, lanes) for s in smooth], 1)
    own = dot(own, out_x[:, :128])
    both = jnp.concatenate([s.reshape(3, 24, lanes) for s in correction], 2)
    c0, c1, c2 = both[0], both[1], both[2]
    five = jnp.concatenate(
        [
            c0,
            0.375 * c0 + 0.75 * c1 - 0.125 * c2,
            c1,
            -0.125 * c0 + 0.75 * c1 + 0.375 * c2,
            c2,
        ],
        0,
    )
    five = dot(five, out_x[:, 128:])
    tall = jnp.concatenate(
        [
            jnp.concatenate([v[24 * z : 24 * z + 24] for z in range(5)], 1)
            for v in (own, five)
        ],
        0,
    )
    result = dot(out_y, tall)
    for z in range(5):
        out_ref[z] = result[0:17, 128 * z : 128 * z + 128]
    for copy in started:
        copy.wait_send()


def solution(mesh):
    gx = mesh.shape["gx"]
    lanes = 64 * gx
    phases = DEG1 + DEG2

    def step(element_load, conductivity):
        vmem = pl.BlockSpec(memory_space=pltpu.VMEM)
        f32 = jnp.float32
        return pl.pallas_call(
            kernel,
            out_shape=jax.ShapeDtypeStruct(element_load.shape, f32),
            in_specs=[vmem, vmem],
            out_specs=vmem,
            scratch_shapes=[
                pltpu.VMEM((gx - 1,) + element_load.shape, f32),
                pltpu.VMEM((gx - 1, 2, 8, 128), f32),
                pltpu.VMEM((2, 8, 128), f32),
                pltpu.VMEM((phases, 2, 4, 3, 8, lanes), f32),
                pltpu.VMEM((phases, 2, 4, 3, 8, lanes), f32),
                pltpu.VMEM((phases, 2, 4, 8, lanes), f32),
                pltpu.VMEM((phases, 2, 4, 8, lanes), f32),
                pltpu.VMEM((phases, 4, 8, lanes), f32),
                pltpu.VMEM((phases, 4, 8, lanes), f32),
                pltpu.SemaphoreType.DMA((phases, 8)),
                pltpu.SemaphoreType.DMA((phases, 8)),
                pltpu.SemaphoreType.DMA((2, gx - 1)),
                pltpu.SemaphoreType.DMA((2, gx - 1)),
            ],
            compiler_params=pltpu.CompilerParams(
                collective_id=0, has_side_effects=True, vmem_limit_bytes=48 * 1024 * 1024
            ),
        )(element_load, conductivity)

    spec = P("gz", "gy", "gx")
    return jax.shard_map(
        step, mesh=mesh, in_specs=(spec, spec), out_specs=spec, check_vma=False
    )
```

time: 134 us -> 47.2 us (0.35)
  waiting for transfers between devices: 48.7 us -> 0 us
  Pallas kernels: 0 us -> 44.9 us
  starting transfers between devices: 27.7 us -> 0 us
  local copies, waits for them, and re-layouts: 23.7 us -> 2.15 us
  blocking collectives: 17 us -> 0 us
  other arithmetic: 14.1 us -> 0 us
  between operations: 2.88 us -> 0.01 us
    ppermute x34 -> x0, waiting for transfers between devices: 48.7 us -> none  [the longest x17 27.5 us: padded(): lax.ppermute(tail, axis, [(i, (i + 1) % count) for i in range(count)])]
    pallas_call x0 -> x1, Pallas kernels: none -> 44.9 us  [step(): pl.pallas_call(kernel, out_shape=jax.ShapeDtypeStruct(element_load.shape,...]
    ppermute x34 -> x0, starting transfers between devices: 27.7 us -> none  [the longest x17 17.1 us: padded(): lax.ppermute(tail, axis, [(i, (i + 1) % count) for i in range(count)])]
    all_gather x3 -> x0, blocking collectives: 17 us -> none  [the longest x1 6.98 us: on_device(): lax.all_gather(coarse_diag, 'gx', axis=2, tiled=True)]
    slice x85 -> x0, local copies, waits for them, and re-layouts: 14.6 us -> none  [the longest x12 8.73 us: node_slices(): lax.slice_in_dim(node_field, a, a + 2 * elements - 1, 2, axis=which_axis)]
    add x92 -> x0, other arithmetic: 7.43 us -> none  [the longest x36 1.55 us: contract(): matrix[b][0] * pieces[0] + matrix[b][1] * pieces[1]]
    another operation x52 -> x0, local copies, waits for them, and re-layouts: 4.97 us -> none  [the longest x19 3.67 us: fold_back(): woven_nodes = jnp.stack([even_nodes, middle_part], axis=target + 1)]
    another operation x114 -> x0, other arithmetic: 4.05 us -> none  [the longest x57 1.99 us: fold_back(): woven_nodes = jnp.stack([even_nodes, middle_part], axis=target + 1)]
  transfers between devices with their start and end apart: 34 -> 0, of which waited for: 30 -> 0; matrix products, arithmetic and copies ran while one was open for 2% -> 0% of each run, Pallas kernels for 0% -> 0%
where the time goes in v1:
time: 47.2 us; the launch traced here: 47 us
  Pallas kernels  44.9 us (95%)
  local copies, waits for them, and re-layouts  2.15 us (5%)
    pallas_call x1, Pallas kernels, step(): pl.pallas_call(kernel, out_shape=jax.ShapeDtypeStruct(element_load.shape,...  44.9 us
    unnamed x5, local copies, waits for them, and re-layouts  2.15 us

profile of v1, /device:TPU:0, one launch (start us, length us, event | category | flops | bytes accessed | tf_op | source)
XLA Modules:
  0.0 47.0 jit_solution(407343954026368829)
XLA Ops:
  0.0 0.0 copy-start
  0.0 0.8 %copy-done = f32[5,17,128]{2,1,0:T(8,128)S(1)} copy-done((f32[5,17,128]{2,1,0:T(8,128)S(1)}, f32[5,17,128]{2,1,0:T(8,128)}, u32[]{:S(2)}) %copy-start) | copy-done | bytes 43544
  0.8 0.0 copy-start.1
  0.8 0.7 %copy-done.1 = f32[2,8,64]{2,1,0:T(8,128)S(1)} copy-done((f32[2,8,64]{2,1,0:T(8,128)S(1)}, f32[2,8,64]{2,1,0:T(8,128)}, u32[]{:S(2)}) %copy-start.1) | copy-done | bytes 4120
  1.5 44.9 %shard_map.28 = f32[5,17,128]{2,1,0:T(8,128)S(1)} custom-call(f32[5,17,128]{2,1,0:T(8,128)S(1)} %copy-done, f32[2,8,64]{2,1,0:T(8,128)S(1)} %copy-done.1), custom_call_target="tpu_custom_call" | custom-call | tf_op jit(solution)/shard_map/pallas_call | solution.py:377
  46.4 0.6 %copy.4 = f32[5,17,128]{2,1,0:T(8,128)} copy(f32[5,17,128]{2,1,0:T(8,128)S(1)} %shard_map.28) | data formatting | bytes 87040
Async XLA Ops:
  0.0 0.8 %copy-start = (f32[5,17,128]{2,1,0:T(8,128)S(1)}, f32[5,17,128]{2,1,0:T(8,128)}, u32[]{:S(2)}) copy-start(f32[5,17,128]{2,1,0:T(8,128)} %load_ref.1) | copy-start | bytes 130564
  0.8 0.7 %copy-start.1 = (f32[2,8,64]{2,1,0:T(8,128)S(1)}, f32[2,8,64]{2,1,0:T(8,128)}, u32[]{:S(2)}) copy-start(f32[2,8,64]{2,1,0:T(8,128)} %cond_ref.1) | copy-start | bytes 12292

commit v2 on v1

--- a/solution.py
+++ b/solution.py
@@ -22,8 +22,24 @@
     return lax.broadcasted_iota(jnp.int32, shape, dim)
 
 
-def dot(a, b):
-    return jnp.dot(a, b, precision=lax.Precision.HIGHEST, preferred_element_type=jnp.float32)
+def pieces(v):
+    high = v.astype(jnp.bfloat16).astype(jnp.float32)
+    rest = v - high
+    mid = rest.astype(jnp.bfloat16).astype(jnp.float32)
+    return [high, mid, rest - mid]
+
+
+def dot_right(v, matrix):
+    n = v.shape[0]
+    tall = jnp.concatenate(pieces(v), 0).astype(jnp.bfloat16)
+    out = jnp.dot(tall, matrix, preferred_element_type=jnp.float32)
+    return out[2 * n :] + out[n : 2 * n] + out[:n]
+
+
+def dot_left(matrix, v):
+    tall = jnp.concatenate(pieces(v), 0).astype(jnp.bfloat16)
+    wide = jnp.concatenate([matrix] * 3, 1).astype(jnp.bfloat16)
+    return jnp.dot(wide, tall, preferred_element_type=jnp.float32)
 
 
 def weight(d, odd):
@@ -38,32 +54,50 @@
     return jnp.where(d < -(period // 2), d + period, d)
 
 
-def x_matrices(lanes):
+def bits(n):
+    return n.bit_length() - 1
+
+
+def split_matrix(lanes):
     n = 2 * lanes
     r, c = iota((n, n), 0), iota((n, n), 1)
-    split = jnp.where(r == 2 * (c % lanes) + c // lanes, 1.0, 0.0)
-    q, e = r % 128, (r // 128) * 64 + r % 128
-    hit = ((c < lanes) & (e == c)) | ((c >= lanes) & (e // 2 == c % (lanes // 2)))
-    place = jnp.where((q < 64) & hit, 1.0, 0.0)
-    node = 2 * (r % lanes) + r // lanes
-    cp, m = c // lanes, c % (lanes // 2)
-    restrict = weight(wrapped(node - 4 * m - 2 * cp, n), cp == 1)
+    return jnp.where(r == 2 * (c & (lanes - 1)) + (c >> bits(lanes)), 1.0, 0.0).astype(jnp.bfloat16)
+
+
+def place_matrix(lanes):
+    n = 2 * lanes
+    r, c = iota((n, n), 0), iota((n, n), 1)
+    q, e = r & 127, ((r >> 7) << 6) + (r & 127)
+    hit = ((c < lanes) & (e == c)) | ((c >= lanes) & ((e >> 1) == (c & (lanes // 2 - 1))))
+    return jnp.where((q < 64) & hit, 1.0, 0.0).astype(jnp.bfloat16)
+
+
+def restrict_matrix(lanes):
+    n = 2 * lanes
+    r, c = iota((n, n), 0), iota((n, n), 1)
+    node = 2 * (r & (lanes - 1)) + (r >> bits(lanes))
+    cp, m = c >> bits(lanes), c & (lanes // 2 - 1)
+    return weight(wrapped(node - 4 * m - 2 * cp, n), cp == 1).astype(jnp.bfloat16)
+
+
+def out_matrix(lanes):
+    n = 2 * lanes
     r, c = iota((n, 128), 0), iota((n, 128), 1)
-    merge = jnp.where(2 * (r % lanes) + r // lanes == c, 1.0, 0.0)
-    cp, m = r // lanes, r % lanes
+    m, cp = r & (lanes - 1), r >> bits(lanes)
+    merge = jnp.where(2 * m + cp == c, 1.0, 0.0)
     prolong = jnp.where(
         m < lanes // 2, weight(wrapped(c - 4 * m - 2 * cp, n), cp == 1), 0.0
     )
-    return split, place, restrict, jnp.concatenate([merge, prolong], 1)
+    return jnp.concatenate([merge, prolong], 1).astype(jnp.bfloat16)
 
 
 def fine_row(r):
-    kind, i = r // 8, r % 8
+    kind, i = r >> 3, r & 7
     return jnp.where(kind == 2, jnp.where(i == 7, 16, 1000), 2 * i + kind)
 
 
 def coarse_row(r):
-    kind, i = r // 8, r % 8
+    kind, i = r >> 3, r & 7
     low = jnp.where(i < 4, 4 * i + 2 * kind, -1000)
     return jnp.where(kind == 2, jnp.where(i == 3, 16, -1000), low), kind == 1
 
@@ -145,7 +179,7 @@
     return to_nodes([m * f for m, f in zip(modes, factor)])
 
 
-def exchange(fields, phase, ny, bufs):
+def exchange(fields, phase, ny, bufs, beside=None):
     zs, zr, ys, yr, cs, cr, send_sem, recv_sem = bufs
     flat = [part for field in fields for part in field]
     count = len(flat)
@@ -183,6 +217,8 @@
         )
         copy.start()
         copies.append(copy)
+    if beside is not None:
+        beside()
     for copy in copies:
         copy.wait_recv()
     out = []
@@ -238,7 +274,7 @@
 
 
 def kernel(load_ref, cond_ref, out_ref, line, cells, cell_out, zs, zr, ys, yr, cs, cr,
-           send_sem, recv_sem, x_send, x_recv):
+           send_sem, recv_sem, x_send, x_recv, matrix_x, matrix_out):
     gx, gy, gz = lax.axis_size("gx"), lax.axis_size("gy"), lax.axis_size("gz")
     ix, iy, iz = lax.axis_index("gx"), lax.axis_index("gy"), lax.axis_index("gz")
     lanes = 64 * gx
@@ -271,8 +307,7 @@
             )
             copy.start()
             arrivals.append(copy)
-    split, place, restrict_x, out_x = x_matrices(lanes)
-    restrict_y, out_y = y_matrices()
+    split_x, place = split_matrix(lanes), place_matrix(lanes)
     for copy in arrivals:
         copy.wait_recv()
     started += arrivals
@@ -288,19 +323,25 @@
     joined = jnp.concatenate(
         [rows(load_ref)] + [rows(line.at[d]) for d in range(gx - 1)], 1
     )
-    loads = dot(joined, split)
+    loads = dot_right(joined, split_x)
     load = (loads[:, :lanes].reshape(5, 3, 8, lanes), loads[:, lanes:].reshape(5, 3, 8, lanes))
     joined = jnp.concatenate(
         [cell_out[...].reshape(16, 128)] + [cells[d].reshape(16, 128) for d in range(gx - 1)], 1
     )
-    conds = dot(joined, place)
+    conds = dot_right(joined, place)
     cond = conds[:, :lanes].reshape(2, 8, lanes)
     pair = conds[:8, lanes:] + conds[8:, lanes:]
     r, c = iota((8, 8), 0), iota((8, 8), 1)
-    coarse_cond = dot(jnp.where(c // 2 == r, 0.125, 0.0), pair).reshape(1, 8, lanes)
+    coarse_cond = dot_left(jnp.where((c >> 1) == r, 0.125, 0.0), pair).reshape(1, 8, lanes)
 
     fine = factors(cond, 1.0)
-    (right, diagonal), copies = exchange([load, to_nodes(fine, True)], 0, 8, bufs)
+
+    def fill():
+        matrix_x[...] = restrict_matrix(lanes)
+        matrix_out[...] = out_matrix(lanes)
+
+    (right, diagonal), copies = exchange([load, to_nodes(fine, True)], 0, 8, bufs, fill)
+    restrict_y, out_y = y_matrices()
     started += copies
     smooth, copies = chebyshev(right, diagonal, fine, DEG1, 8, 1, bufs)
     started += copies
@@ -317,8 +358,8 @@
         ],
         0,
     )
-    three = dot(three, restrict_x).reshape(3, 24, 2 * lanes)
-    wide = dot(restrict_y, jnp.concatenate([three[z] for z in range(3)], 1))
+    three = dot_right(three, matrix_x[...]).reshape(3, 24, 2 * lanes)
+    wide = dot_left(restrict_y, jnp.concatenate([three[z] for z in range(3)], 1))
     coarse_load = tuple(
         jnp.stack(
             [
@@ -338,7 +379,7 @@
     started += copies
 
     own = jnp.concatenate([s.reshape(120, lanes) for s in smooth], 1)
-    own = dot(own, out_x[:, :128])
+    own = dot_right(own, matrix_out[:, :128])
     both = jnp.concatenate([s.reshape(3, 24, lanes) for s in correction], 2)
     c0, c1, c2 = both[0], both[1], both[2]
     five = jnp.concatenate(
@@ -351,7 +392,7 @@
         ],
         0,
     )
-    five = dot(five, out_x[:, 128:])
+    five = dot_right(five, matrix_out[:, 128:])
     tall = jnp.concatenate(
         [
             jnp.concatenate([v[24 * z : 24 * z + 24] for z in range(5)], 1)
@@ -359,7 +400,7 @@
         ],
         0,
     )
-    result = dot(out_y, tall)
+    result = dot_left(out_y, tall)
     for z in range(5):
         out_ref[z] = result[0:17, 128 * z : 128 * z + 128]
     for copy in started:
@@ -393,6 +434,8 @@
                 pltpu.SemaphoreType.DMA((phases, 8)),
                 pltpu.SemaphoreType.DMA((2, gx - 1)),
                 pltpu.SemaphoreType.DMA((2, gx - 1)),
+                pltpu.VMEM((2 * lanes, 2 * lanes), jnp.bfloat16),
+                pltpu.VMEM((2 * lanes, 256), jnp.bfloat16),
             ],
             compiler_params=pltpu.CompilerParams(
                 collective_id=0, has_side_effects=True, vmem_limit_bytes=48 * 1024 * 1024

time: 47.2 us -> 46.6 us (0.987)
  Pallas kernels: 44.9 us -> 44.2 us
    pallas_call x1, Pallas kernels: 44.9 us -> 44.2 us  [step(): pl.pallas_call(kernel, out_shape=jax.ShapeDtypeStruct(element_load.shape,...]
where the time goes in v2:
time: 46.6 us; the launch traced here: 46.4 us
  Pallas kernels  44.2 us (95%)
  local copies, waits for them, and re-layouts  2.15 us (5%)
    pallas_call x1, Pallas kernels, step(): pl.pallas_call(kernel, out_shape=jax.ShapeDtypeStruct(element_load.shape,...  44.2 us
    unnamed x5, local copies, waits for them, and re-layouts  2.15 us

profile of v2, /device:TPU:0, one launch (start us, length us, event | category | flops | bytes accessed | tf_op | source)
XLA Modules:
  0.0 46.4 jit_solution(8829744816444374141)
XLA Ops:
  0.0 0.0 copy-start
  0.0 0.8 %copy-done = f32[5,17,128]{2,1,0:T(8,128)S(1)} copy-done((f32[5,17,128]{2,1,0:T(8,128)S(1)}, f32[5,17,128]{2,1,0:T(8,128)}, u32[]{:S(2)}) %copy-start) | copy-done | bytes 43544
  0.8 0.0 copy-start.1
  0.8 0.7 %copy-done.1 = f32[2,8,64]{2,1,0:T(8,128)S(1)} copy-done((f32[2,8,64]{2,1,0:T(8,128)S(1)}, f32[2,8,64]{2,1,0:T(8,128)}, u32[]{:S(2)}) %copy-start.1) | copy-done | bytes 4120
  1.5 44.2 %shard_map.28 = f32[5,17,128]{2,1,0:T(8,128)S(1)} custom-call(f32[5,17,128]{2,1,0:T(8,128)S(1)} %copy-done, f32[2,8,64]{2,1,0:T(8,128)S(1)} %copy-done.1), custom_call_target="tpu_custom_call" | custom-call | tf_op jit(solution)/shard_map/pallas_call | solution.py:418
  45.7 0.6 %copy.4 = f32[5,17,128]{2,1,0:T(8,128)} copy(f32[5,17,128]{2,1,0:T(8,128)S(1)} %shard_map.28) | data formatting | bytes 87040
Async XLA Ops:
  0.0 0.8 %copy-start = (f32[5,17,128]{2,1,0:T(8,128)S(1)}, f32[5,17,128]{2,1,0:T(8,128)}, u32[]{:S(2)}) copy-start(f32[5,17,128]{2,1,0:T(8,128)} %load_ref.1) | copy-start | bytes 130564
  0.8 0.7 %copy-start.1 = (f32[2,8,64]{2,1,0:T(8,128)S(1)}, f32[2,8,64]{2,1,0:T(8,128)}, u32[]{:S(2)}) copy-start(f32[2,8,64]{2,1,0:T(8,128)} %cond_ref.1) | copy-start | bytes 12292

commit v3 on v2

--- a/solution.py
+++ b/solution.py
@@ -74,9 +74,9 @@
 
 def restrict_matrix(lanes):
     n = 2 * lanes
-    r, c = iota((n, n), 0), iota((n, n), 1)
+    r, c = iota((n, lanes), 0), iota((n, lanes), 1)
     node = 2 * (r & (lanes - 1)) + (r >> bits(lanes))
-    cp, m = c >> bits(lanes), c & (lanes // 2 - 1)
+    cp, m = c >> bits(lanes // 2), c & (lanes // 2 - 1)
     return weight(wrapped(node - 4 * m - 2 * cp, n), cp == 1).astype(jnp.bfloat16)
 
 
@@ -96,20 +96,38 @@
     return jnp.where(kind == 2, jnp.where(i == 7, 16, 1000), 2 * i + kind)
 
 
-def coarse_row(r):
-    kind, i = r >> 3, r & 7
-    low = jnp.where(i < 4, 4 * i + 2 * kind, -1000)
-    return jnp.where(kind == 2, jnp.where(i == 3, 16, -1000), low), kind == 1
-
-
-def y_matrices():
+def packet_matrix():
+    r, c = iota((32, 24), 0), iota((32, 24), 1)
+    kind, i = (r & 7) >> 2, r & 3
+    end = r >= 24
+    at = jnp.where(end, 16, 4 * i + 2 * kind)
+    layer = jnp.where(end, r - 24, r >> 3)
+    values = jnp.where(end, weight(fine_row(c) - at, False), weight(fine_row(c) - at, kind == 1))
+    blocks = [jnp.where(layer == l, values, 0.0) for l in range(3)]
+    r, c = iota((32, 8), 0), iota((32, 8), 1)
+    return jnp.concatenate(blocks + [jnp.where((c >> 1) == r - 27, 0.125, 0.0)], 1)
+
+
+def window_matrix():
+    r, c = iota((112, 96), 0), iota((112, 96), 1)
+    l, kind, slot, i = r >> 5, (r & 31) >> 4, (r & 15) >> 2, r & 3
+    at, k = c >> 5, c & 31
+    body = (at == slot) & (k == 8 * l + 4 * kind + i)
+    end = (kind == 0) & (i == 0) & (at == slot - 1) & (k == 24 + l)
+    cells = (at == slot) & (k == 27 + i)
+    return jnp.where(((r < 96) & (body | end)) | ((r >= 96) & cells), 1.0, 0.0)
+
+
+def out_rows():
     r, c = iota((24, 24), 0), iota((24, 24), 1)
-    at, odd = coarse_row(r)
-    restrict = weight(fine_row(c) - at, odd)
-    at, odd = coarse_row(c)
-    prolong = weight(r - at, odd)
     merge = jnp.where(fine_row(c) == r, 1.0, 0.0)
-    return restrict, jnp.concatenate([merge, prolong], 1)
+    r, c = iota((24, 32), 0), iota((24, 32), 1)
+    odd = c >= 16
+    e = c & 15
+    inside = (e >= 4) & (e <= jnp.where(odd, 7, 8))
+    at = 4 * (e - 4) + jnp.where(odd, 2, 0)
+    prolong = jnp.where(inside, weight(r - at, odd), 0.0)
+    return jnp.concatenate([merge, prolong], 1)
 
 
 def roll_x(v, step):
@@ -119,7 +137,7 @@
 
 def roll_y(v, step):
     flat = v.reshape((-1,) + v.shape[-2:])
-    return pltpu.roll(flat, step % 8, 1).reshape(v.shape)
+    return pltpu.roll(flat, step % v.shape[-2], 1).reshape(v.shape)
 
 
 def forward(a, b, c):
@@ -177,6 +195,33 @@
     parts = [jnp.stack([y[:, :, 2 * z + a] for z in range(cells)], 0) for a in range(3)]
     modes = forward(*parts)
     return to_nodes([m * f for m, f in zip(modes, factor)])
+
+
+def window_nodes(modes, squared=False):
+    cells = modes[0].shape[0]
+    low, mid, up = backward(*modes, squared)
+    layers = []
+    for z in range(cells):
+        layers += [low[z] + up[z - 1], mid[z]]
+    q = jnp.stack(layers, 0)
+    low, mid, up = backward(q[:, 0], q[:, 1], q[:, 2], squared)
+    q = jnp.stack([low + roll_y(up, 1), mid], 2)
+    low, mid, up = backward(q[:, 0], q[:, 1], q[:, 2], squared)
+    return low + roll_x(up, 1), mid
+
+
+def apply_window(field, factor):
+    even, odd = field
+    cells = factor[0].shape[0]
+    g = jnp.stack(forward(even, odd, roll_x(even, -1)), 0)
+    low, mid = g[:, :, 0], g[:, :, 1]
+    y = jnp.stack(forward(low, mid, roll_y(low, -1)), 0)
+    parts = [
+        jnp.stack([y[:, :, (2 * z + a) % (2 * cells)] for z in range(cells)], 0)
+        for a in range(3)
+    ]
+    modes = forward(*parts)
+    return window_nodes([m * f for m, f in zip(modes, factor)])
 
 
 def exchange(fields, phase, ny, bufs, beside=None):
@@ -251,18 +296,15 @@
     return jnp.concatenate([whole, end], 1)
 
 
-def chebyshev(right, diagonal, factor, degree, ny, phase, bufs):
+def chebyshev(right, scaled, operate, degree):
     centre = 0.5 * (UPPER + LOWER)
     half = 0.5 * (UPPER - LOWER)
     sharp = centre / half
     f = 1.0 / sharp
-    scaled = [inverse(d, ny) for d in diagonal]
     update = [s * r * (1.0 / centre) for s, r in zip(scaled, right)]
     total = update
-    started = []
     for k in range(1, degree):
-        (image,), copies = exchange([apply_local(total, factor, ny)], phase + k - 1, ny, bufs)
-        started += copies
+        image = operate(total, k)
         g = 1.0 / (2.0 * sharp - f)
         update = [
             (g * f) * u + (2.0 * g / half) * (s * (r - a))
@@ -270,29 +312,38 @@
         ]
         total = [t + u for t, u in zip(total, update)]
         f = g
-    return total, started
+    return total
 
 
 def kernel(load_ref, cond_ref, out_ref, line, cells, cell_out, zs, zr, ys, yr, cs, cr,
-           send_sem, recv_sem, x_send, x_recv, matrix_x, matrix_out):
+           send_sem, recv_sem, x_send, x_recv, matrix_x, matrix_out,
+           packets, w_send, w_recv):
     gx, gy, gz = lax.axis_size("gx"), lax.axis_size("gy"), lax.axis_size("gz")
     ix, iy, iz = lax.axis_index("gx"), lax.axis_index("gy"), lax.axis_index("gz")
     lanes = 64 * gx
     bufs = (zs, zr, ys, yr, cs, cr, send_sem, recv_sem)
     barrier = pltpu.get_barrier_semaphore()
-    for dy, dz in STEPS:
-        pl.semaphore_signal(
-            barrier, inc=1,
-            device_id={"gy": lax.rem(iy + dy + gy, gy), "gz": lax.rem(iz + dz + gz, gz)},
-            device_id_type=MESH,
-        )
+    wide_z = packets.shape[0]
+    own_z = wide_z // 2
+    slots = [
+        (z, y) for z in range(wide_z) for y in range(3) if (z, y) != (own_z, 1)
+    ]
+
+    def holder(slot):
+        return {
+            "gy": lax.rem(iy + 1 - slot[1] + gy, gy),
+            "gz": lax.rem(iz + own_z - slot[0] + gz, gz),
+        }
+
+    for slot in slots:
+        pl.semaphore_signal(barrier, inc=1, device_id=holder(slot), device_id_type=MESH)
     for d in range(1, gx):
         pl.semaphore_signal(
             barrier, inc=1, device_id={"gx": lax.rem(ix + d, gx)}, device_id_type=MESH
         )
     cell_out[...] = jnp.zeros(cell_out.shape, jnp.float32)
     cell_out[:, :, 0:64] = cond_ref[...]
-    pl.semaphore_wait(barrier, len(STEPS) + gx - 1)
+    pl.semaphore_wait(barrier, len(slots) + gx - 1)
     started = []
     arrivals = []
     for d in range(1, gx):
@@ -331,8 +382,6 @@
     conds = dot_right(joined, place)
     cond = conds[:, :lanes].reshape(2, 8, lanes)
     pair = conds[:8, lanes:] + conds[8:, lanes:]
-    r, c = iota((8, 8), 0), iota((8, 8), 1)
-    coarse_cond = dot_left(jnp.where((c >> 1) == r, 0.125, 0.0), pair).reshape(1, 8, lanes)
 
     fine = factors(cond, 1.0)
 
@@ -341,10 +390,14 @@
         matrix_out[...] = out_matrix(lanes)
 
     (right, diagonal), copies = exchange([load, to_nodes(fine, True)], 0, 8, bufs, fill)
-    restrict_y, out_y = y_matrices()
     started += copies
-    smooth, copies = chebyshev(right, diagonal, fine, DEG1, 8, 1, bufs)
-    started += copies
+
+    def operate(field, k):
+        (image,), copies = exchange([apply_local(field, fine, 8)], k, 8, bufs)
+        started.extend(copies)
+        return image
+
+    smooth = chebyshev(right, [inverse(d, 8) for d in diagonal], operate, DEG1)
     image = apply_local(smooth, fine, 8)
     part = [
         jnp.concatenate([(b - a).reshape(5, 24, lanes) for b, a in zip(load, image)], 2)
@@ -358,30 +411,47 @@
         ],
         0,
     )
-    three = dot_right(three, matrix_x[...]).reshape(3, 24, 2 * lanes)
-    wide = dot_left(restrict_y, jnp.concatenate([three[z] for z in range(3)], 1))
-    coarse_load = tuple(
-        jnp.stack(
-            [
-                wide[:, (2 * z + p) * lanes : (2 * z + p + 1) * lanes].reshape(3, 8, lanes)
-                for z in range(3)
-            ],
-            0,
+    three = dot_right(three, matrix_x[...])
+    packets[own_z, 1] = dot_left(packet_matrix(), jnp.concatenate([three, pair], 0))
+    copies = []
+    for slot in slots:
+        copy = pltpu.make_async_remote_copy(
+            src_ref=packets.at[own_z, 1],
+            dst_ref=packets.at[slot],
+            send_sem=w_send.at[slot],
+            recv_sem=w_recv.at[slot],
+            device_id=holder(slot),
+            device_id_type=MESH,
         )
-        for p in range(2)
-    )
-    coarse = factors(coarse_cond, 2.0)
-    (right, diagonal), copies = exchange(
-        [coarse_load, to_nodes(coarse, True)], DEG1, 4, bufs
-    )
+        copy.start()
+        copies.append(copy)
     started += copies
-    correction, copies = chebyshev(right, diagonal, coarse, DEG2, 4, DEG1 + 1, bufs)
-    started += copies
-
     own = jnp.concatenate([s.reshape(120, lanes) for s in smooth], 1)
     own = dot_right(own, matrix_out[:, :128])
-    both = jnp.concatenate([s.reshape(3, 24, lanes) for s in correction], 2)
-    c0, c1, c2 = both[0], both[1], both[2]
+    gather = window_matrix()
+    for copy in copies:
+        copy.wait_recv()
+    tall = [
+        jnp.concatenate([packets[z, y] for y in range(3)], 0) for z in range(wide_z)
+    ]
+    tall = dot_left(gather, jnp.concatenate(tall, 1))
+    tall = [tall[:, z * lanes : (z + 1) * lanes] for z in range(wide_z)]
+    layers = []
+    for z in range(wide_z):
+        layers += [tall[z][0:32] + tall[z - 1][64:96], tall[z][32:64]]
+    packed = jnp.stack(layers, 0).reshape(2 * wide_z, 2, 16, lanes)
+    turned = roll_x(packed, lanes // 2)
+    first = iota(packed.shape[-2:], 1) < lanes // 2
+    right = (jnp.where(first, packed, turned), jnp.where(first, turned, packed))
+    coarse = factors(jnp.stack([t[96:112] for t in tall], 0), 2.0)
+    diagonal = window_nodes(coarse, True)
+    correction = chebyshev(
+        right, [1.0 / d for d in diagonal], lambda v, k: apply_window(v, coarse), DEG2
+    )
+    c0, c1, c2 = (
+        jnp.concatenate([v[(2 * own_z + l) % (2 * wide_z)].reshape(32, lanes) for v in correction], 1)
+        for l in range(3)
+    )
     five = jnp.concatenate(
         [
             c0,
@@ -395,12 +465,12 @@
     five = dot_right(five, matrix_out[:, 128:])
     tall = jnp.concatenate(
         [
-            jnp.concatenate([v[24 * z : 24 * z + 24] for z in range(5)], 1)
-            for v in (own, five)
+            jnp.concatenate([v[n * z : n * z + n] for z in range(5)], 1)
+            for v, n in ((own, 24), (five, 32))
         ],
         0,
     )
-    result = dot_left(out_y, tall)
+    result = dot_left(out_rows(), tall)
     for z in range(5):
         out_ref[z] = result[0:17, 128 * z : 128 * z + 128]
     for copy in started:
@@ -410,7 +480,8 @@
 def solution(mesh):
     gx = mesh.shape["gx"]
     lanes = 64 * gx
-    phases = DEG1 + DEG2
+    phases = DEG1
+    wide_z = min(mesh.shape["gz"], 9)
 
     def step(element_load, conductivity):
         vmem = pl.BlockSpec(memory_space=pltpu.VMEM)
@@ -434,8 +505,11 @@
                 pltpu.SemaphoreType.DMA((phases, 8)),
                 pltpu.SemaphoreType.DMA((2, gx - 1)),
                 pltpu.SemaphoreType.DMA((2, gx - 1)),
-                pltpu.VMEM((2 * lanes, 2 * lanes), jnp.bfloat16),
+                pltpu.VMEM((2 * lanes, lanes), jnp.bfloat16),
                 pltpu.VMEM((2 * lanes, 256), jnp.bfloat16),
+                pltpu.VMEM((wide_z, 3, 32, lanes), f32),
+                pltpu.SemaphoreType.DMA((wide_z, 3)),
+                pltpu.SemaphoreType.DMA((wide_z, 3)),
             ],
             compiler_params=pltpu.CompilerParams(
                 collective_id=0, has_side_effects=True, vmem_limit_bytes=48 * 1024 * 1024

time: 46.6 us -> 35.4 us (0.76)
  Pallas kernels: 44.2 us -> 32.9 us
    pallas_call x1, Pallas kernels: 44.2 us -> 32.9 us  [step(): pl.pallas_call(kernel, out_shape=jax.ShapeDtypeStruct(element_load.shape,...]
where the time goes in v3:
time: 35.4 us; the launch traced here: 35 us
  Pallas kernels  32.9 us (93%)
  local copies, waits for them, and re-layouts  2.15 us (6%)
    pallas_call x1, Pallas kernels, step(): pl.pallas_call(kernel, out_shape=jax.ShapeDtypeStruct(element_load.shape,...  32.9 us
    unnamed x5, local copies, waits for them, and re-layouts  2.15 us

profile of v3, /device:TPU:0, one launch (start us, length us, event | category | flops | bytes accessed | tf_op | source)
XLA Modules:
  0.0 35.0 jit_solution(14091606453423616538)
XLA Ops:
  0.0 0.0 copy-start
  0.0 0.8 %copy-done = f32[5,17,128]{2,1,0:T(8,128)S(1)} copy-done((f32[5,17,128]{2,1,0:T(8,128)S(1)}, f32[5,17,128]{2,1,0:T(8,128)}, u32[]{:S(2)}) %copy-start) | copy-done | bytes 43544
  0.8 0.0 copy-start.1
  0.8 0.7 %copy-done.1 = f32[2,8,64]{2,1,0:T(8,128)S(1)} copy-done((f32[2,8,64]{2,1,0:T(8,128)S(1)}, f32[2,8,64]{2,1,0:T(8,128)}, u32[]{:S(2)}) %copy-start.1) | copy-done | bytes 4120
  1.5 32.9 %shard_map.28 = f32[5,17,128]{2,1,0:T(8,128)S(1)} custom-call(f32[5,17,128]{2,1,0:T(8,128)S(1)} %copy-done, f32[2,8,64]{2,1,0:T(8,128)S(1)} %copy-done.1), custom_call_target="tpu_custom_call" | custom-call | tf_op jit(solution)/shard_map/pallas_call | solution.py:489
  34.4 0.6 %copy.4 = f32[5,17,128]{2,1,0:T(8,128)} copy(f32[5,17,128]{2,1,0:T(8,128)S(1)} %shard_map.28) | data formatting | bytes 87040
Async XLA Ops:
  0.0 0.8 %copy-start = (f32[5,17,128]{2,1,0:T(8,128)S(1)}, f32[5,17,128]{2,1,0:T(8,128)}, u32[]{:S(2)}) copy-start(f32[5,17,128]{2,1,0:T(8,128)} %load_ref.1) | copy-start | bytes 130564
  0.8 0.7 %copy-start.1 = (f32[2,8,64]{2,1,0:T(8,128)S(1)}, f32[2,8,64]{2,1,0:T(8,128)}, u32[]{:S(2)}) copy-start(f32[2,8,64]{2,1,0:T(8,128)} %cond_ref.1) | copy-start | bytes 12292

commit v4 on v3

--- a/solution.py
+++ b/solution.py
@@ -65,11 +65,11 @@
 
 
 def place_matrix(lanes):
-    n = 2 * lanes
-    r, c = iota((n, n), 0), iota((n, n), 1)
-    q, e = r & 127, ((r >> 7) << 6) + (r & 127)
-    hit = ((c < lanes) & (e == c)) | ((c >= lanes) & ((e >> 1) == (c & (lanes // 2 - 1))))
-    return jnp.where((q < 64) & hit, 1.0, 0.0).astype(jnp.bfloat16)
+    r, c = iota((2 * lanes, 3 * lanes), 0), iota((2 * lanes, 3 * lanes), 1)
+    layer, e = (r >> 6) & 1, ((r >> 7) << 6) + (r & 63)
+    block, at = c >> bits(lanes), c & (lanes - 1)
+    hit = ((block == layer) & (e == at)) | ((block == 2) & ((e >> 1) == (at & (lanes // 2 - 1))))
+    return jnp.where(hit, 1.0, 0.0).astype(jnp.bfloat16)
 
 
 def restrict_matrix(lanes):
@@ -289,6 +289,29 @@
     return [(out[2 * i], out[2 * i + 1]) for i in range(len(fields))], copies
 
 
+def fine_diagonal(cells, below, above):
+    row = iota(cells.shape[-2:], 0)
+    mass, stiff = (4.0 / 30.0, 16.0 / 30.0), (7.0 / 3.0, 16.0 / 3.0)
+    out = []
+    for x in range(2):
+        v, lo, hi = cells, below, above
+        if x == 0:
+            v, lo, hi = (t + roll_x(t, 1) for t in (v, lo, hi))
+        rows = ((v + jnp.where(row == 0, lo, roll_y(v, 1)), 0), (v, 1), (v + hi, 0))
+        parts = []
+        for z in range(5):
+            for t, y in rows:
+                near = t[z // 2 + 1] if z % 2 else t[z // 2] + t[z // 2 + 1]
+                k = (x, y, z % 2)
+                m = [mass[i] for i in k]
+                w = [stiff[i] for i in k]
+                share = w[0] * m[1] * m[2] + m[0] * w[1] * m[2] + m[0] * m[1] * w[2]
+                count = 2 ** (3 - sum(k))
+                parts.append(near * share + REACTION * m[0] * m[1] * m[2] * count)
+        out.append(jnp.stack(parts, 0).reshape((5, 3) + cells.shape[1:]))
+    return out
+
+
 def inverse(diagonal, ny):
     row = iota(diagonal.shape[-2:], 0)
     whole = jnp.where(row < ny, 1.0 / diagonal[:, 0:2], 0.0)
@@ -317,7 +340,7 @@
 
 def kernel(load_ref, cond_ref, out_ref, line, cells, cell_out, zs, zr, ys, yr, cs, cr,
            send_sem, recv_sem, x_send, x_recv, matrix_x, matrix_out,
-           packets, w_send, w_recv):
+           packets, w_send, w_recv, near, far, n_send, n_recv, summed):
     gx, gy, gz = lax.axis_size("gx"), lax.axis_size("gy"), lax.axis_size("gz")
     ix, iy, iz = lax.axis_index("gx"), lax.axis_index("gy"), lax.axis_index("gz")
     lanes = 64 * gx
@@ -335,15 +358,34 @@
             "gz": lax.rem(iz + own_z - slot[0] + gz, gz),
         }
 
+    def beside(step, d):
+        return {
+            "gx": lax.rem(ix + d, gx),
+            "gy": lax.rem(iy + step[0] + gy, gy),
+            "gz": lax.rem(iz + step[1] + gz, gz),
+        }
+
     for slot in slots:
         pl.semaphore_signal(barrier, inc=1, device_id=holder(slot), device_id_type=MESH)
+    for step in STEPS:
+        for d in range(1, gx):
+            pl.semaphore_signal(barrier, inc=1, device_id=beside(step, d), device_id_type=MESH)
     for d in range(1, gx):
         pl.semaphore_signal(
             barrier, inc=1, device_id={"gx": lax.rem(ix + d, gx)}, device_id_type=MESH
         )
-    cell_out[...] = jnp.zeros(cell_out.shape, jnp.float32)
-    cell_out[:, :, 0:64] = cond_ref[...]
-    pl.semaphore_wait(barrier, len(slots) + gx - 1)
+    cell_out[:, 0:64] = cond_ref[0]
+    cell_out[:, 64:128] = cond_ref[1]
+    for k, (dy, dz) in enumerate(STEPS):
+        y, z = (16 if dy == 1 else 0), (4 if dz == 1 else 0)
+        if dy == 0:
+            near[k, 0:17] = load_ref[z]
+            near[k, 24:32] = cell_out[...]
+        else:
+            for l in range(5) if dz == 0 else (0,):
+                near[k, l : l + 1] = load_ref[l if dz == 0 else z, y : y + 1]
+            near[k, 5:6] = cell_out[7:8] if dy == 1 else cell_out[0:1]
+    pl.semaphore_wait(barrier, len(slots) + 9 * (gx - 1))
     started = []
     arrivals = []
     for d in range(1, gx):
@@ -358,6 +400,21 @@
             )
             copy.start()
             arrivals.append(copy)
+    for k in (4, 5, 6, 7, 2, 3, 0, 1):
+        count = 32 if STEPS[k][0] == 0 else 8
+        for d in range(gx):
+            copy = pltpu.make_async_remote_copy(
+                src_ref=near.at[k, pl.ds(0, count)],
+                dst_ref=far.at[k, (gx - d) % gx, pl.ds(0, count)],
+                send_sem=n_send.at[k, d],
+                recv_sem=n_recv.at[k, (gx - d) % gx],
+                device_id=beside(STEPS[k], d),
+                device_id_type=MESH,
+            )
+            copy.start()
+            arrivals.append(copy)
+    matrix_x[...] = restrict_matrix(lanes)
+    matrix_out[...] = out_matrix(lanes)
     split_x, place = split_matrix(lanes), place_matrix(lanes)
     for copy in arrivals:
         copy.wait_recv()
@@ -371,29 +428,61 @@
             parts.append(jnp.broadcast_to(ref[z, 16:17, :], (8, 128)))
         return jnp.concatenate(parts, 0)
 
+    bricks = [load_ref] + [line.at[d] for d in range(gx - 1)]
+    for g, brick in enumerate(bricks):
+        for z in range(5):
+            v = brick[z]
+            first, end = far[0, g, z : z + 1], far[1, g, z : z + 1]
+            if z == 0:
+                v = v + far[2, g, 0:17]
+                first, end = first + far[4, g, 0:1], end + far[6, g, 0:1]
+            if z == 4:
+                v = v + far[3, g, 0:17]
+                first, end = first + far[5, g, 0:1], end + far[7, g, 0:1]
+            summed[g, z] = v
+            summed[g, z, 0:1] = v[0:1] + first
+            summed[g, z, 16:17] = v[16:17] + end
     joined = jnp.concatenate(
-        [rows(load_ref)] + [rows(line.at[d]) for d in range(gx - 1)], 1
-    )
-    loads = dot_right(joined, split_x)
-    load = (loads[:, :lanes].reshape(5, 3, 8, lanes), loads[:, lanes:].reshape(5, 3, 8, lanes))
+        [
+            jnp.concatenate([rows(b) for b in bricks], 1),
+            jnp.concatenate([rows(summed.at[g]) for g in range(gx)], 1),
+        ],
+        0,
+    )
+    loads = dot_right(joined, split_x).reshape(2, 5, 3, 8, 2 * lanes)
+    load, right = (
+        (loads[i, :, :, :, :lanes], loads[i, :, :, :, lanes:]) for i in range(2)
+    )
+    owned = [cell_out] + [cells.at[d] for d in range(gx - 1)]
     joined = jnp.concatenate(
-        [cell_out[...].reshape(16, 128)] + [cells[d].reshape(16, 128) for d in range(gx - 1)], 1
+        [
+            jnp.concatenate(
+                [owned[g][...], far[2, g, 24:32], far[3, g, 24:32]]
+                + [far[k, g, 0:8] for k in (0, 1, 4, 5, 6, 7)],
+                0,
+            )
+            for g in range(gx)
+        ],
+        1,
     )
     conds = dot_right(joined, place)
-    cond = conds[:, :lanes].reshape(2, 8, lanes)
-    pair = conds[:8, lanes:] + conds[8:, lanes:]
-
+
+    def one(at, layer):
+        row = conds[at + 5 : at + 6, layer * lanes : (layer + 1) * lanes]
+        return jnp.broadcast_to(row, (8, lanes))
+
+    cond = jnp.stack([conds[0:8, :lanes], conds[0:8, lanes : 2 * lanes]], 0)
+    around = jnp.stack(
+        [conds[8:16, lanes : 2 * lanes], cond[0], cond[1], conds[16:24, :lanes]], 0
+    )
+    below = jnp.stack([one(40, 1), one(24, 0), one(24, 1), one(48, 0)], 0)
+    above = jnp.stack([one(56, 1), one(32, 0), one(32, 1), one(64, 0)], 0)
+    pair = conds[0:8, 2 * lanes :]
     fine = factors(cond, 1.0)
-
-    def fill():
-        matrix_x[...] = restrict_matrix(lanes)
-        matrix_out[...] = out_matrix(lanes)
-
-    (right, diagonal), copies = exchange([load, to_nodes(fine, True)], 0, 8, bufs, fill)
-    started += copies
+    diagonal = fine_diagonal(around, below, above)
 
     def operate(field, k):
-        (image,), copies = exchange([apply_local(field, fine, 8)], k, 8, bufs)
+        (image,), copies = exchange([apply_local(field, fine, 8)], k - 1, 8, bufs)
         started.extend(copies)
         return image
 
@@ -480,7 +569,7 @@
 def solution(mesh):
     gx = mesh.shape["gx"]
     lanes = 64 * gx
-    phases = DEG1
+    phases = DEG1 - 1
     wide_z = min(mesh.shape["gz"], 9)
 
     def step(element_load, conductivity):
@@ -493,12 +582,12 @@
             out_specs=vmem,
             scratch_shapes=[
                 pltpu.VMEM((gx - 1,) + element_load.shape, f32),
-                pltpu.VMEM((gx - 1, 2, 8, 128), f32),
-                pltpu.VMEM((2, 8, 128), f32),
-                pltpu.VMEM((phases, 2, 4, 3, 8, lanes), f32),
-                pltpu.VMEM((phases, 2, 4, 3, 8, lanes), f32),
-                pltpu.VMEM((phases, 2, 4, 8, lanes), f32),
-                pltpu.VMEM((phases, 2, 4, 8, lanes), f32),
+                pltpu.VMEM((gx - 1, 8, 128), f32),
+                pltpu.VMEM((8, 128), f32),
+                pltpu.VMEM((phases, 2, 2, 3, 8, lanes), f32),
+                pltpu.VMEM((phases, 2, 2, 3, 8, lanes), f32),
+                pltpu.VMEM((phases, 2, 2, 8, lanes), f32),
+                pltpu.VMEM((phases, 2, 2, 8, lanes), f32),
                 pltpu.VMEM((phases, 4, 8, lanes), f32),
                 pltpu.VMEM((phases, 4, 8, lanes), f32),
                 pltpu.SemaphoreType.DMA((phases, 8)),
@@ -510,6 +599,11 @@
                 pltpu.VMEM((wide_z, 3, 32, lanes), f32),
                 pltpu.SemaphoreType.DMA((wide_z, 3)),
                 pltpu.SemaphoreType.DMA((wide_z, 3)),
+                pltpu.VMEM((8, 32, 128), f32),
+                pltpu.VMEM((8, gx, 32, 128), f32),
+                pltpu.SemaphoreType.DMA((8, gx)),
+                pltpu.SemaphoreType.DMA((8, gx)),
+                pltpu.VMEM((gx,) + element_load.shape, f32),
             ],
             compiler_params=pltpu.CompilerParams(
                 collective_id=0, has_side_effects=True, vmem_limit_bytes=48 * 1024 * 1024

time: 35.4 us -> 32.7 us (0.924)
  Pallas kernels: 32.9 us -> 30.4 us
    pallas_call x1, Pallas kernels: 32.9 us -> 30.4 us  [step(): pl.pallas_call(kernel, out_shape=jax.ShapeDtypeStruct(element_load.shape,...]
where the time goes in v4:
time: 32.7 us; the launch traced here: 32.5 us
  Pallas kernels  30.4 us (93%)
  local copies, waits for them, and re-layouts  2.15 us (7%)
    pallas_call x1, Pallas kernels, step(): pl.pallas_call(kernel, out_shape=jax.ShapeDtypeStruct(element_load.shape,...  30.4 us
    unnamed x5, local copies, waits for them, and re-layouts  2.15 us

profile of v4, /device:TPU:0, one launch (start us, length us, event | category | flops | bytes accessed | tf_op | source)
XLA Modules:
  0.0 32.5 jit_solution(6997528638729665499)
XLA Ops:
  0.0 0.0 copy-start
  0.0 0.8 %copy-done = f32[5,17,128]{2,1,0:T(8,128)S(1)} copy-done((f32[5,17,128]{2,1,0:T(8,128)S(1)}, f32[5,17,128]{2,1,0:T(8,128)}, u32[]{:S(2)}) %copy-start) | copy-done | bytes 43544
  0.8 0.0 copy-start.1
  0.8 0.7 %copy-done.1 = f32[2,8,64]{2,1,0:T(8,128)S(1)} copy-done((f32[2,8,64]{2,1,0:T(8,128)S(1)}, f32[2,8,64]{2,1,0:T(8,128)}, u32[]{:S(2)}) %copy-start.1) | copy-done | bytes 4120
  1.5 30.4 %shard_map.28 = f32[5,17,128]{2,1,0:T(8,128)S(1)} custom-call(f32[5,17,128]{2,1,0:T(8,128)S(1)} %copy-done, f32[2,8,64]{2,1,0:T(8,128)S(1)} %copy-done.1), custom_call_target="tpu_custom_call" | custom-call | tf_op jit(solution)/shard_map/pallas_call | solution.py:578
  31.9 0.6 %copy.4 = f32[5,17,128]{2,1,0:T(8,128)} copy(f32[5,17,128]{2,1,0:T(8,128)S(1)} %shard_map.28) | data formatting | bytes 87040
Async XLA Ops:
  0.0 0.8 %copy-start = (f32[5,17,128]{2,1,0:T(8,128)S(1)}, f32[5,17,128]{2,1,0:T(8,128)}, u32[]{:S(2)}) copy-start(f32[5,17,128]{2,1,0:T(8,128)} %load_ref.1) | copy-start | bytes 130564
  0.8 0.7 %copy-start.1 = (f32[2,8,64]{2,1,0:T(8,128)S(1)}, f32[2,8,64]{2,1,0:T(8,128)}, u32[]{:S(2)}) copy-start(f32[2,8,64]{2,1,0:T(8,128)} %cond_ref.1) | copy-start | bytes 12292

commit v5 on v4

--- a/solution.py
+++ b/solution.py
@@ -232,8 +232,9 @@
     last = layers - 1
     row = iota(flat[0].shape[-2:], 0)
     for f, part in enumerate(flat):
-        zs[phase, 0, f] = part[last]
-        zs[phase, 1, f] = part[0]
+        for d, l in enumerate((last, 0)):
+            zs[phase, d, 2 * f : 2 * f + 2] = part[l, 0:2]
+            zs[phase, d, 4, f : f + 1] = part[l, 2, ny - 1 : ny]
         for l in range(layers):
             ys[phase, 0, f, l : l + 1] = part[l, 2, ny - 1 : ny]
             ys[phase, 1, f, l : l + 1] = part[l, 0, 0:1]
@@ -249,7 +250,7 @@
         if k < 2:
             src, dst = ys.at[phase, k, pl.ds(0, count)], yr.at[phase, k, pl.ds(0, count)]
         elif k < 4:
-            src, dst = zs.at[phase, k - 2, pl.ds(0, count)], zr.at[phase, k - 2, pl.ds(0, count)]
+            src, dst = zs.at[phase, k - 2], zr.at[phase, k - 2]
         else:
             src, dst = cs.at[phase, k - 4], cr.at[phase, k - 4]
         copy = pltpu.make_async_remote_copy(
@@ -278,13 +279,13 @@
             if l == 0:
                 first = first + cr[phase, 0, f : f + 1]
                 end = end + cr[phase, 2, f : f + 1]
-            low = part[l, 0] + jnp.where(row == 0, first, 0.0)
-            layer = jnp.stack([low, part[l, 1], part[l, 2] + end], 0)
-            if l == 0:
-                layer = layer + zr[phase, 0, f]
-            if l == last:
-                layer = layer + zr[phase, 1, f]
-            done.append(layer)
+            low, mid = part[l, 0], part[l, 1]
+            if l in (0, last):
+                d = 0 if l == 0 else 1
+                end = end + zr[phase, d, 4, f : f + 1]
+                low, mid = low + zr[phase, d, 2 * f], mid + zr[phase, d, 2 * f + 1]
+            low = low + jnp.where(row == 0, first, 0.0)
+            done.append(jnp.stack([low, mid, part[l, 2] + end], 0))
         out.append(jnp.stack(done, 0))
     return [(out[2 * i], out[2 * i + 1]) for i in range(len(fields))], copies
 
@@ -584,8 +585,8 @@
                 pltpu.VMEM((gx - 1,) + element_load.shape, f32),
                 pltpu.VMEM((gx - 1, 8, 128), f32),
                 pltpu.VMEM((8, 128), f32),
-                pltpu.VMEM((phases, 2, 2, 3, 8, lanes), f32),
-                pltpu.VMEM((phases, 2, 2, 3, 8, lanes), f32),
+                pltpu.VMEM((phases, 2, 5, 8, lanes), f32),
+                pltpu.VMEM((phases, 2, 5, 8, lanes), f32),
                 pltpu.VMEM((phases, 2, 2, 8, lanes), f32),
                 pltpu.VMEM((phases, 2, 2, 8, lanes), f32),
                 pltpu.VMEM((phases, 4, 8, lanes), f32),

time: 32.7 us -> 32.3 us (0.988)
  Pallas kernels: 30.4 us -> 29.9 us
    pallas_call x1, Pallas kernels: 30.4 us -> 29.9 us  [step(): pl.pallas_call(kernel, out_shape=jax.ShapeDtypeStruct(element_load.shape,...]
where the time goes in v5:
time: 32.3 us; the launch traced here: 32.1 us
  Pallas kernels  29.9 us (93%)
  local copies, waits for them, and re-layouts  2.15 us (7%)
    pallas_call x1, Pallas kernels, step(): pl.pallas_call(kernel, out_shape=jax.ShapeDtypeStruct(element_load.shape,...  29.9 us
    unnamed x5, local copies, waits for them, and re-layouts  2.15 us

profile of v5, /device:TPU:0, one launch (start us, length us, event | category | flops | bytes accessed | tf_op | source)
XLA Modules:
  0.0 32.1 jit_solution(17185609680375593112)
XLA Ops:
  0.0 0.0 copy-start
  0.0 0.8 %copy-done = f32[5,17,128]{2,1,0:T(8,128)S(1)} copy-done((f32[5,17,128]{2,1,0:T(8,128)S(1)}, f32[5,17,128]{2,1,0:T(8,128)}, u32[]{:S(2)}) %copy-start) | copy-done | bytes 43544
  0.8 0.0 copy-start.1
  0.8 0.7 %copy-done.1 = f32[2,8,64]{2,1,0:T(8,128)S(1)} copy-done((f32[2,8,64]{2,1,0:T(8,128)S(1)}, f32[2,8,64]{2,1,0:T(8,128)}, u32[]{:S(2)}) %copy-start.1) | copy-done | bytes 4120
  1.5 29.9 %shard_map.28 = f32[5,17,128]{2,1,0:T(8,128)S(1)} custom-call(f32[5,17,128]{2,1,0:T(8,128)S(1)} %copy-done, f32[2,8,64]{2,1,0:T(8,128)S(1)} %copy-done.1), custom_call_target="tpu_custom_call" | custom-call | tf_op jit(solution)/shard_map/pallas_call | solution.py:579
  31.5 0.6 %copy.4 = f32[5,17,128]{2,1,0:T(8,128)} copy(f32[5,17,128]{2,1,0:T(8,128)S(1)} %shard_map.28) | data formatting | bytes 87040
Async XLA Ops:
  0.0 0.8 %copy-start = (f32[5,17,128]{2,1,0:T(8,128)S(1)}, f32[5,17,128]{2,1,0:T(8,128)}, u32[]{:S(2)}) copy-start(f32[5,17,128]{2,1,0:T(8,128)} %load_ref.1) | copy-start | bytes 130564
  0.8 0.7 %copy-start.1 = (f32[2,8,64]{2,1,0:T(8,128)S(1)}, f32[2,8,64]{2,1,0:T(8,128)}, u32[]{:S(2)}) copy-start(f32[2,8,64]{2,1,0:T(8,128)} %cond_ref.1) | copy-start | bytes 12292
